TPU v7x, 256 devices: a whole 4x4x8 slice. The times are simulated.
256 devices in a mesh: gx: 32 (over y, x, core), gy: 8 (over z).
Axes of the slice: x: 4, y: 4, z: 8, core: 2. Of those that a mesh axis runs over, the one named last changes fastest.
Arguments:
- corpus: bfloat16 [262144, 1024], P(('gx', 'gy')), may hold values from -6 to 6
- rotation: bfloat16 [1024, 1024], replicated, may hold values from -0.1875 to 0.1875
- code_table: int32 [262144, 64], P(('gx', 'gy')), may hold values from 0 to 255
- codebooks: bfloat16 [64, 256, 16], replicated, may hold values from -6 to 6
Outputs:
- new_rotation: float32 [1024, 1024], P('gx')
- distortion: float32 [262144], P(('gx', 'gy'))
All inputs are finite; a program needn't handle non-finite values.
Results may differ from a plain program's by a relative error of at most 0.0003.
Values sent between devices are 32-bit elements; how exact they have to be, the bound alone decides.
No kernel may reach another device: no remote copies, remote signals or barrier semaphores. Data moves between devices by JAX's collectives and lax.ppermute only.
A program may use at most 64 MiB of HBM per device.

v0:
```python
import math

import jax
import jax.numpy as jnp
from jax import lax
from jax.sharding import PartitionSpec as P

ITERS = 4


highest = lax.Precision.HIGHEST


def rows_times_whole(left_rows, whole_matrix):
    return lax.dot_general(left_rows, whole_matrix, (((1,), (1,)), ((), ())), precision=highest)


def collect(owned_rows):
    return lax.all_gather(owned_rows, "gx", axis=0, tiled=True)


def body(corpus, rotation, code_table, codebooks):
    row_count = corpus.shape[0]
    model_width = corpus.shape[1]
    sub_count = codebooks.shape[0]
    word_count = codebooks.shape[1]
    sub_width = codebooks.shape[2]
    group_count = sub_count // 8
    group_codes = code_table.reshape(row_count, group_count, 8).transpose(1, 0, 2)
    group_books = codebooks.reshape(group_count, 8, word_count, sub_width)
    word_index = lax.iota(jnp.int32, word_count)
    slot_index = lax.iota(jnp.int32, 8)
    diagonal_mask = slot_index[:, None, None, None] == slot_index[None, None, :, None]

    def rebuild(state_in, inputs_pair):
        block_codes, books_block = inputs_pair
        onehot = (block_codes[:, :, None] == word_index[None, None, :]).astype(jnp.bfloat16)
        onehot = onehot.reshape(row_count, 8 * word_count)
        spread = jnp.where(diagonal_mask, books_block[:, :, None, :], jnp.zeros((), jnp.bfloat16))
        block_books = spread.reshape(8 * word_count, 8 * sub_width)
        section = jnp.dot(onehot, block_books, preferred_element_type=jnp.float32)
        return (state_in, section.astype(jnp.bfloat16))

    _, pieces = lax.scan(rebuild, 0, (group_codes, group_books))
    rebuilt = pieces.transpose(1, 0, 2).reshape(row_count, model_width)
    rotated = jnp.dot(corpus, rotation, preferred_element_type=jnp.float32)
    mismatch = rotated - rebuilt.astype(jnp.float32)
    distortion = jnp.sum(mismatch * mismatch, axis=1)
    size_gx = lax.axis_size("gx")
    size_gy = lax.axis_size("gy")
    row_scale = 1.0 / math.sqrt(row_count * size_gx * size_gy)
    term = lax.dot_general(
        corpus, rebuilt, (((0,), (0,)), ((), ())), preferred_element_type=jnp.float32
    )
    summed = lax.psum(term * row_scale, "gy")
    owned = lax.psum_scatter(summed, "gx", scatter_dimension=0, tiled=True)
    whole_matrix = collect(owned)
    products = rows_times_whole(owned, whole_matrix)
    square_sum = lax.psum(jnp.sum(products * products), "gx")
    factor = (square_sum + 1e-06) ** (-0.25)
    current = owned * factor
    whole_matrix = whole_matrix * factor
    for iteration in range(ITERS):
        if iteration > 0:
            whole_matrix = collect(current)
        gram_rows = rows_times_whole(current, whole_matrix)
        current = 1.5 * current - 0.5 * jnp.dot(gram_rows, whole_matrix, precision=highest)
    return (current * math.sqrt(model_width), distortion)


def solution(mesh):
    return jax.shard_map(
        body,
        mesh=mesh,
        in_specs=(P(("gx", "gy"), None), P(), P(("gx", "gy"), None), P()),
        out_specs=(P("gx", None), P(("gx", "gy"))),
        check_vma=False,
    )
```

profile of v0, /device:TPU:1, one launch (start us, length us, event | category | flops | bytes accessed | tf_op | source)
XLA Modules:
  0.0 575.2 jit_solution(17390611191373075243)
XLA Ops:
  7.2 66.0 %while.11 = (s32[]{:T(128)}, bf16[8,1024,128]{2,1,0:T(8,128)(2,1)}, s32[8,1024,8]{1,2,0:T(8,128)}, bf16[8,8,256,16]{2,3,1,0:T(8,128)(2,1)}, s32[]{:T(128)}) while((s32[]{:T(128)}, bf16[8,1024,128]{2,1,0:T(8,128)(2,1)}, s32[8,1024,8]{1,2,0:T(8,128)}, bf16[8,8,256,16]{2,3,1,0:T(8,128)(2,1)}, s32[]{:T(128)}) %tuple.43), condition=%wide.region_1.2_spmd.clone, body=%wide.region_0.1_spmd.clone.sunk | while | flops 539361344 | bytes 11239761 | solution.py:44
  9.5 2.8 iota_compare_fusion.3
  17.7 2.8 iota_compare_fusion.3
  26.0 2.8 iota_compare_fusion.3
  73.3 3.9 copy.24
  77.2 5.9 %multiply_bitcast_fusion = f32[1024,1024]{0,1:T(8,128)} fusion(bf16[1024,1024]{0,1:T(8,128)(2,1)} %bitcast.71, bf16[1024,1024]{1,0:T(8,128)(2,1)S(1)} %copy-done), kind=kOutput, calls=%fused_computation.12 | convolution fusion | flops 2148532224 | bytes 8388608 | tf_op jit(solution)/shard_map/dot_general | solution.py:52
  83.1 5.4 copy.26
  88.5 91.8 %reduce-scatter.4.cloned.1.call-done = f32[32,1024]{1,0:T(8,128)} async-done(((f32[1024,1024]{1,0:T(8,128)}), f32[32,1024]{1,0:T(8,128)}) %reduce-scatter.4.cloned.1.call-update) | async-done | bytes 131088 | tf_op jit(solution)/shard_map/reduce_scatter | solution.py:56
  180.4 70.3 %all-reduce.2.cloned.1.call-done = f32[32,1024]{1,0:T(8,128)} async-done(((f32[32,1024]{1,0:T(8,128)}), f32[32,1024]{1,0:T(8,128)}) %all-reduce.2.cloned.1.call-update) | async-done | bytes 131088 | tf_op jit(solution)/shard_map/psum | solution.py:55
  250.8 57.5 %all-gather.5.cloned.1.call-done = f32[1024,1024]{1,0:T(8,128)} async-done(((f32[32,1024]{1,0:T(8,128)}), f32[1024,1024]{1,0:T(8,128)}) %all-gather.5.cloned.1.call-update) | async-done | bytes 4194320 | tf_op jit(solution)/shard_map/all_gather | solution.py:19
  308.3 6.7 %fusion.23 = f32[]{:T(128)} fusion(f32[32,1024]{1,0:T(8,128)} %all-reduce.2.cloned.1.call-done, f32[1024,1024]{1,0:T(8,128)} %all-gather.5.cloned.1.call-done), kind=kOutput, calls=%fused_computation.29 | convolution fusion | flops 402718720 | bytes 4325380 | tf_op jit(solution)/shard_map/dot_general | solution.py:15
  315.0 63.1 %psum.15 = f32[]{:T(128)} all-reduce(f32[]{:T(128)} %fusion.23), channel_id=1, replica_groups=mesh['gx'=32,'gy'=8] {'gx'}, use_global_device_ids=true, to_apply=%region_5.6 | all-reduce | flops 1 | bytes 8 | tf_op jit(solution)/shard_map/psum | solution.py:59
  378.8 6.1 %fusion.9 = f32[32,1024]{1,0:T(8,128)S(1)} fusion(f32[1024,1024]{1,0:T(8,128)} %all-gather.5.cloned.1.call-done, f32[]{:T(128)S(6)} %pow.3, f32[32,1024]{1,0:T(8,128)S(1)} %copy-done.5), kind=kOutput, calls=%fused_computation.15 | convolution fusion | flops 403734528 | bytes 4456452 | tf_op jit(solution)/shard_map/dot_general | solution.py:15
  384.9 3.2 fusion.16
  388.3 50.5 %all-gather.7.cloned.1.call-done = f32[1024,1024]{1,0:T(8,128)} async-done(((f32[32,1024]{1,0:T(8,128)}), f32[1024,1024]{1,0:T(8,128)}) %all-gather.7.cloned.1.call-update) | async-done | bytes 4194320 | tf_op jit(solution)/shard_map/all_gather | solution.py:19
  438.8 6.2 %fusion.26 = f32[32,1024]{1,0:T(8,128)S(1)} fusion(f32[32,1024]{1,0:T(8,128)} %fusion.16, f32[1024,1024]{1,0:T(8,128)} %all-gather.7.cloned.1.call-done), kind=kOutput, calls=%fused_computation.32 | convolution fusion | flops 402653184 | bytes 4456448 | tf_op jit(solution)/shard_map/dot_general | solution.py:15
  445.1 3.1 fusion.22
  448.5 50.4 %all-gather.9.cloned.1.call-done = f32[1024,1024]{1,0:T(8,128)} async-done(((f32[32,1024]{1,0:T(8,128)}), f32[1024,1024]{1,0:T(8,128)}) %all-gather.9.cloned.1.call-update) | async-done | bytes 4194320 | tf_op jit(solution)/shard_map/all_gather | solution.py:19
  498.9 6.2 %fusion.27 = f32[32,1024]{1,0:T(8,128)S(1)} fusion(f32[32,1024]{1,0:T(8,128)} %fusion.22, f32[1024,1024]{1,0:T(8,128)} %all-gather.9.cloned.1.call-done), kind=kOutput, calls=%fused_computation.33 | convolution fusion | flops 402653184 | bytes 4456448 | tf_op jit(solution)/shard_map/dot_general | solution.py:15
  505.2 3.2 fusion.21
  508.4 5.5 multiply_reduce_fusion
  513.8 45.2 %all-gather.11.cloned.1.call-done = f32[1024,1024]{1,0:T(8,128)} async-done(((f32[32,1024]{1,0:T(8,128)}), f32[1024,1024]{1,0:T(8,128)}) %all-gather.11.cloned.1.call-update) | async-done | bytes 4194320 | tf_op jit(solution)/shard_map/all_gather | solution.py:19
  559.0 6.2 %fusion.28 = f32[32,1024]{1,0:T(8,128)S(1)} fusion(f32[32,1024]{1,0:T(8,128)S(1)} %copy-done.8, f32[1024,1024]{1,0:T(8,128)} %all-gather.11.cloned.1.call-done), kind=kOutput, calls=%fused_computation.34 | convolution fusion | flops 402653184 | bytes 4456448 | tf_op jit(solution)/shard_map/dot_general | solution.py:15
  565.2 3.1 fusion.20
  (116 shorter events, 58.0 us)
Async XLA Ops:
  7.2 70.0 %copy-start = (bf16[1024,1024]{1,0:T(8,128)(2,1)S(1)}, bf16[1024,1024]{1,0:T(8,128)(2,1)}, u32[]{:S(2)}) copy-start(bf16[1024,1024]{1,0:T(8,128)(2,1)} %param.6) | copy-start | bytes 6291460
  7.2 173.2 %reduce-scatter.4.cloned.1.call-start = ((), (), s32[]{:S(2)}) async-start(), calls=%async_computation.6 | async-start | bytes 4325376 | tf_op jit(solution)/shard_map/reduce_scatter | solution.py:56
  88.5 162.2 %all-reduce.2.cloned.1.call-start = ((), (), s32[]{:S(2)}) async-start(), calls=%async_computation.5 | async-start | bytes 262144 | tf_op jit(solution)/shard_map/psum | solution.py:55
  180.4 127.9 %all-gather.5.cloned.1.call-start = ((), (), s32[]{:S(2)}) async-start(), calls=%async_computation.1 | async-start | bytes 4325376 | tf_op jit(solution)/shard_map/all_gather | solution.py:19
  250.7 128.1 %copy-start.5 = (f32[32,1024]{1,0:T(8,128)S(1)}, f32[32,1024]{1,0:T(8,128)}, u32[]{:S(2)}) copy-start(f32[32,1024]{1,0:T(8,128)} %all-reduce.2.cloned.1.call-done) | copy-start | bytes 393220
  250.7 188.1 %all-gather.7.cloned.1.call-start = ((), (), s32[]{:S(2)}) async-start(), calls=%async_computation.2 | async-start | bytes 4325376 | tf_op jit(solution)/shard_map/all_gather | solution.py:19
  378.8 6.2 %copy-start.1 = (f32[1024,1024]{1,0:T(8,128)S(1)}, f32[1024,1024]{1,0:T(8,128)}, u32[]{:S(2)}) copy-start(f32[1024,1024]{1,0:T(8,128)} %all-gather.5.cloned.1.call-done) | copy-start | bytes 12582916
  388.2 56.9 %copy-start.6 = (f32[32,1024]{1,0:T(8,128)S(1)}, f32[32,1024]{1,0:T(8,128)}, u32[]{:S(2)}) copy-start(f32[32,1024]{1,0:T(8,128)} %fusion.16) | copy-start | bytes 393220
  388.2 110.7 %all-gather.9.cloned.1.call-start = ((), (), s32[]{:S(2)}) async-start(), calls=%async_computation.3 | async-start | bytes 4325376 | tf_op jit(solution)/shard_map/all_gather | solution.py:19
  438.8 6.3 %copy-start.2 = (f32[1024,1024]{1,0:T(8,128)S(1)}, f32[1024,1024]{1,0:T(8,128)}, u32[]{:S(2)}) copy-start(f32[1024,1024]{1,0:T(8,128)} %all-gather.7.cloned.1.call-done) | copy-start | bytes 12582916
  448.2 56.9 %copy-start.7 = (f32[32,1024]{1,0:T(8,128)S(1)}, f32[32,1024]{1,0:T(8,128)}, u32[]{:S(2)}) copy-start(f32[32,1024]{1,0:T(8,128)} %fusion.22) | copy-start | bytes 393220
  448.2 110.8 %all-gather.11.cloned.1.call-start = ((), (), s32[]{:S(2)}) async-start(), calls=%async_computation.4 | async-start | bytes 4325376 | tf_op jit(solution)/shard_map/all_gather | solution.py:19
  498.9 6.3 %copy-start.3 = (f32[1024,1024]{1,0:T(8,128)S(1)}, f32[1024,1024]{1,0:T(8,128)}, u32[]{:S(2)}) copy-start(f32[1024,1024]{1,0:T(8,128)} %all-gather.9.cloned.1.call-done) | copy-start | bytes 12582916
  508.4 50.7 %copy-start.8 = (f32[32,1024]{1,0:T(8,128)S(1)}, f32[32,1024]{1,0:T(8,128)}, u32[]{:S(2)}) copy-start(f32[32,1024]{1,0:T(8,128)} %fusion.21) | copy-start | bytes 393220
  559.0 6.2 %copy-start.4 = (f32[1024,1024]{1,0:T(8,128)S(1)}, f32[1024,1024]{1,0:T(8,128)}, u32[]{:S(2)}) copy-start(f32[1024,1024]{1,0:T(8,128)} %all-gather.11.cloned.1.call-done) | copy-start | bytes 12582916
Sparse Core Ops, SparseCore 0:
  88.6 91.7 reduce-scatter.3
  182.7 67.9 all-reduce.1
  253.3 54.9 all-gather.4
  388.3 50.4 all-gather.6
  448.4 50.5 all-gather.8
  508.5 50.5 all-gather.10
where the time goes:
time: 576 us; the launch traced here: 575 us
  waiting for transfers between devices  366 us (64%)
  matrix products  71.3 us (12%)
  blocking collectives  63.1 us (11%)
  local copies, waits for them, and re-layouts  36.3 us (6%)
  other arithmetic  23 us (4%)
  between operations  14.9 us (3%)
    all_gather x4, waiting for transfers between devices, collect(): return lax.all_gather(owned_rows, 'gx', axis=0, tiled=True)  204 us
    reduce_scatter x1, waiting for transfers between devices, body(): owned = lax.psum_scatter(summed, 'gx', scatter_dimension=0, tiled=True)  91.8 us
    psum x1, waiting for transfers between devices, body(): summed = lax.psum(term * row_scale, 'gy')  70.3 us
    psum x1, blocking collectives, body(): square_sum = lax.psum(jnp.sum(products * products), 'gx')  63.1 us
    dot_general x5, matrix products, rows_times_whole(): lax.dot_general(left_rows, whole_matrix, (((1,), (1,)), ((), ())), precis...  31.5 us
    eq x8, other arithmetic, rebuild(): block_codes[:, :, None] == word_index[None, None, :]  22.1 us
    dot_general x8, matrix products, rebuild(): section = jnp.dot(onehot, block_books, preferred_element_type=jnp.float32)  15.7 us
    dot_general x4, matrix products, body(): jnp.dot(gram_rows, whole_matrix, precision=highest)  12.7 us
  transfers between devices with their start and end apart: 6, of which 6 were waited for; matrix products, arithmetic and copies ran while one was open for 1% of the time, Pallas kernels for 0%

commit v1 on v0

v1 whole, which is shorter than its diff:
```python
import math, functools
import jax, jax.numpy as jnp
from jax import lax
from jax.sharding import PartitionSpec as P
from jax.experimental import pallas as pl
from jax.experimental.pallas import tpu as pltpu

BF, F32 = jnp.bfloat16, jnp.float32
MIB = 1 << 20

def split(x):
    hi = x.astype(BF)
    return hi, (x - hi.astype(F32)).astype(BF)

def nt(a, b):
    return lax.dot_general(a, b, (((1,), (1,)), ((), ())), preferred_element_type=F32)

def nn(a, b):
    return lax.dot_general(a, b, (((1,), (0,)), ((), ())), preferred_element_type=F32)

def cross_kernel(scale, half_ref, codes_ref, books_ref, corpus_ref, out_ref, reb_ref):
    subs, width, words = books_ref.shape
    rows = codes_ref.shape[1]
    word = lax.broadcasted_iota(jnp.int16, (words, rows), 0)
    codes = codes_ref[...].astype(jnp.int16)
    one, zero = jnp.ones((), BF), jnp.zeros((), BF)
    for s in range(subs):
        hot = jnp.where(word == codes[s:s + 1, :], one, zero)
        reb_ref[s * width:(s + 1) * width, :] = nn(books_ref[s], hot).astype(BF)
    out_ref[...] = nn(reb_ref[...], corpus_ref[...]) * scale

def cross_half(half, codes_t, books_t, corpus, scale, chunk=16):
    subs, width, words = books_t.shape
    rows, d = corpus.shape
    steps = subs // 2 // chunk
    return pl.pallas_call(
        functools.partial(cross_kernel, scale),
        grid_spec=pltpu.PrefetchScalarGridSpec(
            num_scalar_prefetch=1, grid=(steps,),
            in_specs=[pl.BlockSpec((chunk, rows), lambda i, h: (h[0] * steps + i, 0)),
                      pl.BlockSpec((chunk, width, words), lambda i, h: (h[0] * steps + i, 0, 0)),
                      pl.BlockSpec((rows, d), lambda i, h: (0, 0))],
            out_specs=[pl.BlockSpec((chunk * width, d), lambda i, h: (i, 0)),
                       pl.BlockSpec((chunk * width, rows), lambda i, h: (i, 0))]),
        out_shape=[jax.ShapeDtypeStruct((subs // 2 * width, d), F32),
                   jax.ShapeDtypeStruct((subs // 2 * width, rows), BF)],
        compiler_params=pltpu.CompilerParams(vmem_limit_bytes=40 * MIB),
        name="cross_half",
    )(half, codes_t, books_t, corpus)

def dist_kernel(half_ref, rot_ref, corpus_ref, reb_ref, out_ref):
    rotated = lax.dot_general(rot_ref[...], corpus_ref[...], (((0,), (1,)), ((), ())), preferred_element_type=F32)
    gap = rotated - reb_ref[...].astype(F32)
    out_ref[...] = jnp.sum(gap * gap, axis=0, keepdims=True)

def dist_half(half, rotation, corpus, reb):
    d = rotation.shape[0]
    rows = corpus.shape[0]
    cols = reb.shape[0]
    return pl.pallas_call(
        dist_kernel,
        grid_spec=pltpu.PrefetchScalarGridSpec(
            num_scalar_prefetch=1, grid=(1,),
            in_specs=[pl.BlockSpec((d, cols), lambda i, h: (0, h[0])),
                      pl.BlockSpec((rows, d), lambda i, h: (0, 0)),
                      pl.BlockSpec((cols, rows), lambda i, h: (0, 0))],
            out_specs=pl.BlockSpec((1, rows), lambda i, h: (0, 0))),
        out_shape=jax.ShapeDtypeStruct((1, rows), F32),
        compiler_params=pltpu.CompilerParams(vmem_limit_bytes=40 * MIB),
        name="dist_half",
    )(half, rotation, corpus, reb)

def polar_kernel(place_ref, own_ref, oth_ref, out_ref, yh, yl, gh, gl, th, tl, gf, tf):
    n = yh.shape[0]
    half = n // 2
    blk = 256
    nb = n // blk
    h, l = split(own_ref[...])
    yh[:half, :] = h
    yl[:half, :] = l
    h, l = split(oth_ref[...])
    yh[half:, :] = h
    yl[half:, :] = l

    def spans(i):
        return slice(i * blk, (i + 1) * blk), slice(i * blk, n)

    def put(dh, dl, i, val):
        r, c = spans(i)
        h, l = split(val)
        dh[r, c] = h
        dl[r, c] = l
        for j in range(i + 1, nb):
            t = val[:, (j - i) * blk:(j - i + 1) * blk].T
            h, l = split(t)
            dh[j * blk:(j + 1) * blk, r] = h
            dl[j * blk:(j + 1) * blk, r] = l

    def sym(lh, ll, rh, rl, i):
        r, c = spans(i)
        a, b = lh[r, :], ll[r, :]
        return nn(a, rh[:, c]) + (nn(a, rl[:, c]) + nn(b, rh[:, c]))

    total = jnp.zeros((), F32)
    for i in range(nb):
        r, c = spans(i)
        a, b = yh[r, :], yl[r, :]
        g = nt(a, yh[c, :]) + (nt(a, yl[c, :]) + nt(b, yh[c, :]))
        gf[r, c] = g
        put(gh, gl, i, g)
        sq = g * g
        total = total + 2.0 * jnp.sum(sq) - jnp.sum(sq[:, :blk])
    base = jnp.full((8, 128), total + 1e-06, F32)
    root = lax.rsqrt(base)
    f2 = jnp.max(root)
    f1 = jnp.max(jnp.sqrt(root))

    def thin(ah, al, cur):
        h, l = split(cur)
        w = jnp.concatenate([h, l], axis=1)
        p = nn(ah[...], w)
        k = cur.shape[1]
        return p[:, :k] + (p[:, k:] + nn(al[...], h))

    col = pl.multiple_of(place_ref[1] * 128, 128)
    cur = jnp.concatenate([own_ref[:, pl.ds(col, 128)], oth_ref[:, pl.ds(col, 128)]], axis=0) * f1
    cur = 1.5 * cur - (0.5 * f2) * thin(gh, gl, cur)

    def advance(sh, sl, sf, scale, dh, dl, df, mh, ml, mf):
        for i in range(nb):
            r, c = spans(i)
            m = (1.5 * scale) * sf[r, c] - (0.5 * scale * scale) * sym(sh, sl, sh, sl, i)
            mf[r, c] = m
            put(mh, ml, i, m)
        for i in range(nb):
            r, c = spans(i)
            d = 1.5 * mf[r, c] - (0.5 * scale) * sym(mh, ml, sh, sl, i)
            df[r, c] = d
            put(dh, dl, i, d)

    advance(gh, gl, gf, f2, yh, yl, gf, th, tl, tf)
    cur = 1.5 * cur - 0.5 * thin(yh, yl, cur)
    advance(yh, yl, gf, 1.0, gh, gl, gf, th, tl, tf)
    cur = 1.5 * cur - 0.5 * thin(gh, gl, cur)
    u = thin(gh, gl, cur)
    u = 1.5 * u - 0.5 * thin(gh, gl, u)
    u = 1.5 * u - 0.5 * thin(gh, gl, u)
    cur = (1.5 * cur - 0.5 * u) * math.sqrt(n)
    low = place_ref[0]
    flip = cur.T
    tf[:128, :] = flip
    off = pl.multiple_of(place_ref[2] * 32, 32)
    a = tf[pl.ds(off, 32), :half]
    b = tf[pl.ds(off, 32), half:]
    out_ref[:, :half] = jnp.where(low == 0, a, b)
    out_ref[:, half:] = jnp.where(low == 0, b, a)

def polar(place, own, oth):
    half, n = own.shape
    bf = pltpu.VMEM((n, n), BF)
    return pl.pallas_call(
        polar_kernel,
        in_specs=[pl.BlockSpec(memory_space=pltpu.SMEM)] + [pl.BlockSpec(memory_space=pltpu.VMEM)] * 2,
        out_specs=pl.BlockSpec(memory_space=pltpu.VMEM),
        out_shape=jax.ShapeDtypeStruct((32, n), F32),
        scratch_shapes=[bf, bf, bf, bf, bf, bf, pltpu.VMEM((n, n), F32), pltpu.VMEM((n, n), F32)],
        compiler_params=pltpu.CompilerParams(vmem_limit_bytes=48 * MIB),
        name="polar",
    )(place, own, oth)


AXES = ("gx", "gy")
CORES, SIDE, DEPTH = 2, 4, 8


def place_of(y, x, c, z):
    return ((y * SIDE + x) * CORES + c) * DEPTH + z


def ring_pairs(n, odd):
    pairs = [((i + odd) % n, (i + 1 + odd) % n) for i in range(0, n, 2)]
    return [p if k % 2 == 0 else p[::-1] for k, p in enumerate(pairs)]


def cube_groups():
    return [
        [place_of(y, x, c, z) for y in py for x in px for z in pz]
        for c in range(CORES)
        for py in ring_pairs(SIDE, c)
        for px in ring_pairs(SIDE, c)
        for pz in ring_pairs(DEPTH, c)
    ]


def swap(fn):
    return [
        (place_of(y, x, c, z), place_of(*fn(y, x, c, z)))
        for y in range(SIDE) for x in range(SIDE) for c in range(CORES) for z in range(DEPTH)
    ]


def mate(n, odd):
    table = {}
    for i in range(0, n, 2):
        a, b = (i + odd) % n, (i + 1 + odd) % n
        table[a], table[b] = b, a
    return table


def far(c):
    table = {}
    for a, b in ((0, 3), (4, 7), (2, 5), (6, 1)):
        a, b = (a + c) % DEPTH, (b + c) % DEPTH
        table[a], table[b] = b, a
    return table


SWAP_CORE = swap(lambda y, x, c, z: (y, x, 1 - c, z))
SWAP_X = swap(lambda y, x, c, z: (y, mate(SIDE, 1 - c)[x], c, z))
SWAP_Y = swap(lambda y, x, c, z: (mate(SIDE, 1 - c)[y], x, c, z))
SWAP_Z = swap(lambda y, x, c, z: (y, x, c, mate(DEPTH, 1 - c)[z]))
SWAP_FAR = swap(lambda y, x, c, z: (y, x, c, far(c)[z]))


def send(value, pairs):
    return lax.ppermute(value, AXES, pairs)


def reduce_half(value, bit, pairs):
    half = value.shape[0] // 2
    away = lax.dynamic_slice_in_dim(value, (1 - bit) * half, half, 0)
    keep = lax.dynamic_slice_in_dim(value, bit * half, half, 0)
    return keep + send(away, pairs)


def gather_half(value, bit, pairs):
    other = send(value, pairs)
    return jnp.where(bit == 0, jnp.concatenate([value, other]), jnp.concatenate([other, value]))


def body(corpus, rotation, code_table, codebooks):
    rows, d = corpus.shape
    gx = lax.axis_index("gx")
    core = gx % CORES
    bit_x = gx // CORES % 2
    bit_y = gx // CORES // SIDE % 2
    codes_t = code_table.T
    books_t = codebooks.transpose(0, 2, 1)
    scale = 1.0 / math.sqrt(rows * lax.axis_size("gx") * lax.axis_size("gy"))

    far_half, near_half = (1 - core).reshape(1), core.reshape(1)
    far_term, far_words = cross_half(far_half, codes_t, books_t, corpus, scale)
    arrived = send(far_term, SWAP_CORE)
    near_term, near_words = cross_half(near_half, codes_t, books_t, corpus, scale)
    gaps = dist_half(far_half, rotation, corpus, far_words) + dist_half(near_half, rotation, corpus, near_words)

    groups = cube_groups()
    members = len(groups[0])
    summed = (near_term + arrived).reshape(members, -1, d)
    pieces = lax.all_to_all(summed, AXES, 0, 0, axis_index_groups=groups)
    piece = jnp.sum(pieces, axis=0)

    quarter = reduce_half(piece, bit_x, SWAP_X)
    part = reduce_half(quarter, bit_y, SWAP_Y)
    part = part + send(part, SWAP_Z)
    part = part + send(part, SWAP_FAR)
    quarter = gather_half(part, bit_y, SWAP_Y)
    piece = gather_half(quarter, bit_x, SWAP_X)

    own = lax.all_to_all(jnp.broadcast_to(piece[None], (members,) + piece.shape), AXES, 0, 0, axis_index_groups=groups)
    own = own.reshape(-1, d)
    other = send(own, SWAP_CORE)
    place = jnp.stack([core, gx // 4, gx % 4])
    return polar(place, own, other), gaps.reshape(rows)


def solution(mesh):
    return jax.shard_map(
        body,
        mesh=mesh,
        in_specs=(P(("gx", "gy"), None), P(), P(("gx", "gy"), None), P()),
        out_specs=(P("gx", None), P(("gx", "gy"))),
        check_vma=False,
    )
```

time: 576 us -> 136 us (0.24)
  waiting for transfers between devices: 366 us -> 43 us
  matrix products: 71.3 us -> 0 us
  blocking collectives: 63.1 us -> 22.4 us
  Pallas kernels: 0 us -> 40.6 us
  local copies, waits for them, and re-layouts: 36.3 us -> 5.99 us
  other arithmetic: 23 us -> 5.14 us
  starting transfers between devices: 0.46 us -> 17.6 us
  between operations: 14.9 us -> 0.88 us
    all_gather x4 -> x0, waiting for transfers between devices: 204 us -> none  [collect(): return lax.all_gather(owned_rows, 'gx', axis=0, tiled=True)]
    reduce_scatter x1 -> x0, waiting for transfers between devices: 91.8 us -> none  [body(): owned = lax.psum_scatter(summed, 'gx', scatter_dimension=0, tiled=True)]
    dot_general x19 -> x0, matrix products: 71.3 us -> none  [the longest x5 31.5 us: rows_times_whole(): lax.dot_general(left_rows, whole_matrix, (((1,), (1,)), ((), ())), precis...]
    psum x1 -> x0, waiting for transfers between devices: 70.3 us -> none  [body(): summed = lax.psum(term * row_scale, 'gy')]
    psum x1 -> x0, blocking collectives: 63.1 us -> none  [body(): square_sum = lax.psum(jnp.sum(products * products), 'gx')]
    pallas_call x0 -> x5, Pallas kernels: none -> 40.6 us  [the longest x1 30.7 us: polar(): pl.pallas_call(polar_kernel, in_specs=[pl.BlockSpec(memory_space=pltpu.SM...]
    ppermute x0 -> x8, waiting for transfers between devices: none -> 23.5 us  [send(): return lax.ppermute(value, AXES, pairs)]
    all_to_all x0 -> x1, blocking collectives: none -> 22.4 us  [body(): lax.all_to_all(jnp.broadcast_to(piece[None], (members,) + piece.shape), A...]
  transfers between devices with their start and end apart: 6 -> 9, of which waited for: 6 -> 8; matrix products, arithmetic and copies ran while one was open for 1% -> 0% of each run, Pallas kernels for 0% -> 5%
where the time goes in v1:
time: 136 us
  waiting for transfers between devices  43 us (32%)
  Pallas kernels  40.6 us (30%)
  blocking collectives  22.4 us (16%)
  starting transfers between devices  17.6 us (13%)
  local copies, waits for them, and re-layouts  5.99 us (4%)
  other arithmetic  5.14 us (4%)
    pallas_call x1, Pallas kernels, polar(): pl.pallas_call(polar_kernel, in_specs=[pl.BlockSpec(memory_space=pltpu.SM...  30.7 us
    ppermute x8, waiting for transfers between devices, send(): return lax.ppermute(value, AXES, pairs)  23.5 us
    all_to_all x1, blocking collectives, body(): lax.all_to_all(jnp.broadcast_to(piece[None], (members,) + piece.shape), A...  22.4 us
    all_to_all x1, waiting for transfers between devices, body(): pieces = lax.all_to_all(summed, AXES, 0, 0, axis_index_groups=groups)  19.5 us
    all_to_all x1, starting transfers between devices, body(): pieces = lax.all_to_all(summed, AXES, 0, 0, axis_index_groups=groups)  9.76 us
    ppermute x8, starting transfers between devices, send(): return lax.ppermute(value, AXES, pairs)  7.84 us
    pallas_call x2, Pallas kernels, cross_half(): pl.pallas_call(functools.partial(cross_kernel, scale), grid_spec=pltpu.Pr...  7.31 us
    unnamed x20, local copies, waits for them, and re-layouts  5.71 us
  transfers between devices with their start and end apart: 9, of which 8 were waited for; matrix products, arithmetic and copies ran while one was open for 0% of the time, Pallas kernels for 5%

profile of v1, /device:TPU:1, one launch (start us, length us, event | category | flops | bytes accessed | tf_op | source)
XLA Modules:
  0.0 135.7 jit_solution(2900815008155040947)
XLA Ops:
  0.7 1.6 %copy-done = bf16[1024,1024]{1,0:T(8,128)(2,1)S(1)} copy-done((bf16[1024,1024]{1,0:T(8,128)(2,1)S(1)}, bf16[1024,1024]{1,0:T(8,128)(2,1)}, u32[]{:S(2)}) %copy-start) | copy-done | bytes 2097176
  2.2 1.0 copy-done.4
  3.3 0.9 copy-done.6
  4.2 3.6 %cross_half.3 = (f32[512,1024]{1,0:T(8,128)S(1)}, bf16[512,1024]{1,0:T(8,128)(2,1)S(1)}) custom-call(s32[1]{0:T(128)} %bitcast.5.half_ref, s32[64,1024]{1,0:T(8,128)S(1)} %bitcast.11, bf16[64,16,256]{2,1,0:T(8,128)(2,1)S(1)} %bitcast.9, bf16[1024,1024]{1,0:T(8,128)(2,1)S(1)} %copy-done), custom_call_target="tpu_custom_call" | custom-call | tf_op jit(solution)/shard_map/cross_half/pallas_call | solution.py:36
  7.9 3.3 %collective-permute-start = (f32[512,1024]{1,0:T(8,128)S(1)}, f32[512,1024]{1,0:T(8,128)S(1)}, u32[]{:S(2)}, u32[]{:S(2)}) collective-permute-start(f32[512,1024]{1,0:T(8,128)S(1)} %get-tuple-element.7), channel_id=1, source_target_pairs={{0,8},{1,9},{2,10},{3,11},{4,12},{5,13},{6,14},{7,15},{8,0},{9,1},... | collective-permute-start | bytes 6291464 | tf_op jit(solution)/shard_map/ppermute | solution.py:226
  11.2 3.7 %cross_half.2 = (f32[512,1024]{1,0:T(8,128)S(1)}, bf16[512,1024]{1,0:T(8,128)(2,1)S(1)}) custom-call(s32[1]{0:T(128)} %bitcast.half_ref, s32[64,1024]{1,0:T(8,128)S(1)} %bitcast.12, bf16[64,16,256]{2,1,0:T(8,128)(2,1)S(1)} %bitcast.10, bf16[1024,1024]{1,0:T(8,128)(2,1)S(1)} %copy-done.1), custom_call_target="tpu_custom_call" | custom-call | tf_op jit(solution)/shard_map/cross_half/pallas_call | solution.py:36
  15.0 1.7 %add.50 = f32[512,1024]{1,0:T(8,128)} add(f32[512,1024]{1,0:T(8,128)S(1)} %get-tuple-element.6, f32[512,1024]{1,0:T(8,128)S(1)} %collective-permute-done) | non-fusion elementwise | flops 524288 | bytes 6291456 | tf_op jit(solution)/shard_map/add | solution.py:259
  16.7 9.8 %all-to-all-start = ((f32[8,64,1024]{2,1,0:T(8,128)}), f32[8,64,1024]{2,1,0:T(8,128)}, u32[]{:S(2)}, u32[]{:S(2)}) async-start(f32[8,64,1024]{2,1,0:T(8,128)} %bitcast.13), calls=%async_computation | async-start | bytes 4194304 | tf_op jit(solution)/shard_map/all_to_all | solution.py:260
  26.5 19.5 %all-to-all-done = f32[8,64,1024]{2,1,0:T(8,128)} async-done(((f32[8,64,1024]{2,1,0:T(8,128)}), f32[8,64,1024]{2,1,0:T(8,128)}, u32[]{:S(2)}, u32[]{:S(2)}) %all-to-all-start) | async-done | bytes 2097184 | tf_op jit(solution)/shard_map/all_to_all | solution.py:260
  46.0 1.7 %reduce_sum.9 = f32[64,1024]{1,0:T(8,128)S(1)} reduce(f32[8,64,1024]{2,1,0:T(8,128)} %all-to-all-done, f32[]{:T(128)} %constant.71.clone.1), dimensions={0}, to_apply=%region_0.1 | reduce | flops 458752 | bytes 2359300 | tf_op jit(solution)/shard_map/reduce_sum | solution.py:261
  47.9 3.9 %collective-permute-done.1 = f32[32,1024]{1,0:T(8,128)} collective-permute-done((f32[32,1024]{1,0:T(8,128)S(1)}, f32[32,1024]{1,0:T(8,128)}, u32[]{:S(2)}, u32[]{:S(2)}) %collective-permute-start.1) | collective-permute-done | bytes 131104 | tf_op jit(solution)/shard_map/ppermute | solution.py:226
  51.8 0.9 dynamic-slice_add_fusion
  52.8 3.1 %collective-permute-done.2 = f32[16,1024]{1,0:T(8,128)S(1)} collective-permute-done((f32[16,1024]{1,0:T(8,128)S(1)}, f32[16,1024]{1,0:T(8,128)S(1)}, u32[]{:S(2)}, u32[]{:S(2)}) %collective-permute-start.2) | collective-permute-done | bytes 65568 | tf_op jit(solution)/shard_map/ppermute | solution.py:226
  56.0 3.4 %collective-permute-done.3 = f32[16,1024]{1,0:T(8,128)S(1)} collective-permute-done((f32[16,1024]{1,0:T(8,128)S(1)}, f32[16,1024]{1,0:T(8,128)S(1)}, u32[]{:S(2)}, u32[]{:S(2)}) %collective-permute-start.3) | collective-permute-done | bytes 65568 | tf_op jit(solution)/shard_map/ppermute | solution.py:226
  59.9 6.2 %collective-permute-done.4 = f32[16,1024]{1,0:T(8,128)S(1)} collective-permute-done((f32[16,1024]{1,0:T(8,128)S(1)}, f32[16,1024]{1,0:T(8,128)S(1)}, u32[]{:S(2)}, u32[]{:S(2)}) %collective-permute-start.4) | collective-permute-done | bytes 65568 | tf_op jit(solution)/shard_map/ppermute | solution.py:226
  66.2 3.1 %collective-permute-done.5 = f32[16,1024]{1,0:T(8,128)S(1)} collective-permute-done((f32[16,1024]{1,0:T(8,128)S(1)}, f32[16,1024]{1,0:T(8,128)S(1)}, u32[]{:S(2)}, u32[]{:S(2)}) %collective-permute-start.5) | collective-permute-done | bytes 65568 | tf_op jit(solution)/shard_map/ppermute | solution.py:226
  69.4 3.8 %collective-permute-done.6 = f32[32,1024]{1,0:T(8,128)S(1)} collective-permute-done((f32[32,1024]{1,0:T(8,128)S(1)}, f32[32,1024]{1,0:T(8,128)S(1)}, u32[]{:S(2)}, u32[]{:S(2)}) %collective-permute-start.6) | collective-permute-done | bytes 131104 | tf_op jit(solution)/shard_map/ppermute | solution.py:226
  73.5 22.4 %all_to_all.10 = f32[8,64,1024]{2,1,0:T(8,128)} all-to-all(f32[8,64,1024]{2,1,0:T(8,128)S(1)} %broadcast_in_dim.2), channel_id=1, replica_groups={{0,1,16,17,64,65,80,81},{3,2,19,18,67,66,83,82},{4,5,20,21,68,69,84,85}..., dimensions={0} | all-to-all | bytes 4194304 | tf_op jit(solution)/shard_map/all_to_all | solution.py:270
  95.9 3.6 %collective-permute-start.7 = (f32[512,1024]{1,0:T(8,128)}, f32[512,1024]{1,0:T(8,128)}, u32[]{:S(2)}, u32[]{:S(2)}) collective-permute-start(f32[512,1024]{1,0:T(8,128)} %bitcast.7.own_ref), channel_id=1, source_target_pairs={{0,8},{1,9},{2,10},{3,11},{4,12},{5,13},{6,14},{7,15},{8,0},{9,1},... | collective-permute-start | bytes 6291464 | tf_op jit(solution)/shard_map/ppermute | solution.py:226
  99.5 1.6 %copy-done.2 = bf16[1024,1024]{1,0:T(8,128)(2,1)S(1)} copy-done((bf16[1024,1024]{1,0:T(8,128)(2,1)S(1)}, bf16[1024,1024]{1,0:T(8,128)(2,1)}, u32[]{:S(2)}) %copy-start.2) | copy-done | bytes 2097176
  101.1 1.3 dist_half.2
  103.0 1.3 dist_half.3
  104.3 0.6 add.59
  105.0 30.7 %polar.1 = f32[32,1024]{1,0:T(8,128)} custom-call(s32[3]{0:T(128)S(1)} %pad_add_fusion.place_ref, f32[512,1024]{1,0:T(8,128)} %bitcast.7.own_ref, f32[512,1024]{1,0:T(8,128)} %collective-permute-done.7.oth_ref), custom_call_target="tpu_custom_call" | custom-call | tf_op jit(solution)/shard_map/polar/pallas_call | solution.py:161
  (33 shorter events, 2.0 us)
Async XLA Ops:
  0.6 1.6 %copy-start = (bf16[1024,1024]{1,0:T(8,128)(2,1)S(1)}, bf16[1024,1024]{1,0:T(8,128)(2,1)}, u32[]{:S(2)}) copy-start(bf16[1024,1024]{1,0:T(8,128)(2,1)} %corpus_ref.7) | copy-start | bytes 6291460
  2.2 1.0 copy-start.4
  3.3 0.9 copy-start.6
  4.2 7.0 %copy-start.1 = (bf16[1024,1024]{1,0:T(8,128)(2,1)S(1)}, bf16[1024,1024]{1,0:T(8,128)(2,1)}, u32[]{:S(2)}) copy-start(bf16[1024,1024]{1,0:T(8,128)(2,1)} %corpus_ref.7) | copy-start | bytes 6291460
  4.2 7.0 %copy-start.5 = (bf16[64,256,16]{1,2,0:T(8,128)(2,1)S(1)}, bf16[64,256,16]{1,2,0:T(8,128)(2,1)}, u32[]{:S(2)}) copy-start(bf16[64,256,16]{1,2,0:T(8,128)(2,1)} %param.7) | copy-start | bytes 1572868
  4.2 7.0 %copy-start.7 = (s32[1024,64]{0,1:T(8,128)S(1)}, s32[1024,64]{0,1:T(8,128)}, u32[]{:S(2)}) copy-start(s32[1024,64]{0,1:T(8,128)} %param.6) | copy-start | bytes 786436
  7.9 7.1 %collective-permute-start = (f32[512,1024]{1,0:T(8,128)S(1)}, f32[512,1024]{1,0:T(8,128)S(1)}, u32[]{:S(2)}, u32[]{:S(2)}) collective-permute-start(f32[512,1024]{1,0:T(8,128)S(1)} %get-tuple-element.7), channel_id=1, source_target_pairs={{0,8},{1,9},{2,10},{3,11},{4,12},{5,13},{6,14},{7,15},{8,0},{9,1},... | collective-permute-start | bytes 6291464 | tf_op jit(solution)/shard_map/ppermute | solution.py:226
  14.9 1.9 %copy-start.8 = (bf16[512,1024]{1,0:T(8,128)(2,1)}, bf16[512,1024]{1,0:T(8,128)(2,1)S(1)}, u32[]{:S(2)}) copy-start(bf16[512,1024]{1,0:T(8,128)(2,1)S(1)} %get-tuple-element.9.reb_ref) | copy-start | bytes 3145732
  16.7 29.2 %all-to-all-start = ((f32[8,64,1024]{2,1,0:T(8,128)}), f32[8,64,1024]{2,1,0:T(8,128)}, u32[]{:S(2)}, u32[]{:S(2)}) async-start(f32[8,64,1024]{2,1,0:T(8,128)} %bitcast.13), calls=%async_computation | async-start | bytes 4194304 | tf_op jit(solution)/shard_map/all_to_all | solution.py:260
  47.8 4.0 %collective-permute-start.1 = (f32[32,1024]{1,0:T(8,128)S(1)}, f32[32,1024]{1,0:T(8,128)}, u32[]{:S(2)}, u32[]{:S(2)}) collective-permute-start(f32[32,1024]{1,0:T(8,128)S(1)} %constant_dynamic-slice_fusion.1), channel_id=1, source_target_pairs={{0,48},{1,49},{2,50},{3,51},{4,52},{5,53},{6,54},{7,55},{8,24},{9,... | collective-permute-start | bytes 393224 | tf_op jit(solution)/shard_map/ppermute | solution.py:226
  52.7 3.2 %collective-permute-start.2 = (f32[16,1024]{1,0:T(8,128)S(1)}, f32[16,1024]{1,0:T(8,128)S(1)}, u32[]{:S(2)}, u32[]{:S(2)}) collective-permute-start(f32[16,1024]{1,0:T(8,128)S(1)} %constant_dynamic-slice_fusion), channel_id=1, source_target_pairs={{0,192},{1,193},{2,194},{3,195},{4,196},{5,197},{6,198},{7,199},{8... | collective-permute-start | bytes 196616 | tf_op jit(solution)/shard_map/ppermute | solution.py:226
  55.9 3.5 %collective-permute-start.3 = (f32[16,1024]{1,0:T(8,128)S(1)}, f32[16,1024]{1,0:T(8,128)S(1)}, u32[]{:S(2)}, u32[]{:S(2)}) collective-permute-start(f32[16,1024]{1,0:T(8,128)S(1)} %dynamic-slice_add_fusion.1), channel_id=1, source_target_pairs={{0,7},{1,2},{2,1},{3,4},{4,3},{5,6},{6,5},{7,0},{8,9},{9,8},{10,11... | collective-permute-start | bytes 196616 | tf_op jit(solution)/shard_map/ppermute | solution.py:226
  59.4 6.7 %collective-permute-start.4 = (f32[16,1024]{1,0:T(8,128)S(1)}, f32[16,1024]{1,0:T(8,128)S(1)}, u32[]{:S(2)}, u32[]{:S(2)}) collective-permute-start(f32[16,1024]{1,0:T(8,128)S(1)} %add.57), channel_id=1, source_target_pairs={{0,3},{1,6},{2,5},{3,0},{4,7},{5,2},{6,1},{7,4},{8,13},{9,12},{10,... | collective-permute-start | bytes 196616 | tf_op jit(solution)/shard_map/ppermute | solution.py:226
  66.1 3.2 %collective-permute-start.5 = (f32[16,1024]{1,0:T(8,128)S(1)}, f32[16,1024]{1,0:T(8,128)S(1)}, u32[]{:S(2)}, u32[]{:S(2)}) collective-permute-start(f32[16,1024]{1,0:T(8,128)S(1)} %add.58), channel_id=1, source_target_pairs={{0,192},{1,193},{2,194},{3,195},{4,196},{5,197},{6,198},{7,199},{8... | collective-permute-start | bytes 196616 | tf_op jit(solution)/shard_map/ppermute | solution.py:226
  69.3 3.9 %collective-permute-start.6 = (f32[32,1024]{1,0:T(8,128)S(1)}, f32[32,1024]{1,0:T(8,128)S(1)}, u32[]{:S(2)}, u32[]{:S(2)}) collective-permute-start(f32[32,1024]{1,0:T(8,128)S(1)} %maximum_select_fusion.1), channel_id=1, source_target_pairs={{0,48},{1,49},{2,50},{3,51},{4,52},{5,53},{6,54},{7,55},{8,24},{9,... | collective-permute-start | bytes 393224 | tf_op jit(solution)/shard_map/ppermute | solution.py:226
  95.9 9.0 %collective-permute-start.7 = (f32[512,1024]{1,0:T(8,128)}, f32[512,1024]{1,0:T(8,128)}, u32[]{:S(2)}, u32[]{:S(2)}) collective-permute-start(f32[512,1024]{1,0:T(8,128)} %bitcast.7.own_ref), channel_id=1, source_target_pairs={{0,8},{1,9},{2,10},{3,11},{4,12},{5,13},{6,14},{7,15},{8,0},{9,1},... | collective-permute-start | bytes 6291464 | tf_op jit(solution)/shard_map/ppermute | solution.py:226
  99.5 1.6 %copy-start.2 = (bf16[1024,1024]{1,0:T(8,128)(2,1)S(1)}, bf16[1024,1024]{1,0:T(8,128)(2,1)}, u32[]{:S(2)}) copy-start(bf16[1024,1024]{1,0:T(8,128)(2,1)} %rot_ref.3) | copy-start | bytes 6291460
  101.1 1.6 %copy-start.3 = (bf16[1024,1024]{1,0:T(8,128)(2,1)S(1)}, bf16[1024,1024]{1,0:T(8,128)(2,1)}, u32[]{:S(2)}) copy-start(bf16[1024,1024]{1,0:T(8,128)(2,1)} %rot_ref.3) | copy-start | bytes 6291460
  101.1 1.9 %copy-start.9 = (bf16[512,1024]{1,0:T(8,128)(2,1)S(1)}, bf16[512,1024]{1,0:T(8,128)(2,1)}, u32[]{:S(2)}) copy-start(bf16[512,1024]{1,0:T(8,128)(2,1)} %copy-done.8) | copy-start | bytes 3145732

commit v2 on v1

v2 whole, which is shorter than its diff:
```python
import math, functools
import numpy as np
import jax, jax.numpy as jnp
from jax import lax
from jax.sharding import PartitionSpec as P
from jax.experimental import pallas as pl
from jax.experimental.pallas import tpu as pltpu

BF, F32 = jnp.bfloat16, jnp.float32
MIB = 1 << 20
BLK = 256
ITERS = 4
CHUNK = 16

def split(x):
    hi = x.astype(BF)
    return hi, (x - hi.astype(F32)).astype(BF)

def nt(a, b):
    return lax.dot_general(a, b, (((1,), (1,)), ((), ())), preferred_element_type=F32)

def nn(a, b):
    return lax.dot_general(a, b, (((1,), (0,)), ((), ())), preferred_element_type=F32)

def rebuild(codes, books, words, row, word_at):
    subs = words.shape[0] // books.shape[1]
    width = books.shape[1]
    word = lax.broadcasted_iota(jnp.int16, (books.shape[2], codes.shape[1]), 0)
    one, zero = jnp.ones((), BF), jnp.zeros((), BF)
    for block in range(subs // CHUNK):
        picks = codes[pl.ds(row + block * CHUNK, CHUNK), :].astype(jnp.int16)
        for k in range(CHUNK):
            s = block * CHUNK + k
            hot = jnp.where(word == picks[k:k + 1, :], one, zero)
            words[s * width:(s + 1) * width, :] = nn(books[word_at + s], hot).astype(BF)


def first_kernel(scale, half_ref, codes_hbm, books_hbm, corpus_hbm, out, words_hbm, codes, books, corpus, words, sems):
    subs = books.shape[0]
    first = pl.multiple_of(half_ref[0] * subs, subs)
    loads = [
        pltpu.make_async_copy(codes_hbm.at[pl.ds(first, subs)], codes, sems.at[0]),
        pltpu.make_async_copy(books_hbm.at[pl.ds(first, subs)], books, sems.at[1]),
        pltpu.make_async_copy(corpus_hbm, corpus, sems.at[2]),
    ]
    for load in loads:
        load.start()
    loads[0].wait()
    loads[1].wait()
    rebuild(codes, books, words, 0, 0)
    stores = [pltpu.make_async_copy(words, words_hbm, sems.at[3])]
    stores[0].start()
    loads[2].wait()
    for k in range(corpus.shape[1] // BLK):
        c = slice(k * BLK, (k + 1) * BLK)
        out[:, c] = nn(words[...], corpus[:, c]) * scale
    stores[0].wait()


def cross_first(half, codes_t, books_t, corpus, scale):
    subs, width, size = books_t.shape
    rows, d = corpus.shape
    part = subs // 2
    return pl.pallas_call(
        functools.partial(first_kernel, scale),
        in_specs=[pl.BlockSpec(memory_space=pltpu.SMEM)] + [pl.BlockSpec(memory_space=pl.ANY)] * 3,
        out_specs=[pl.BlockSpec(memory_space=pltpu.VMEM), pl.BlockSpec(memory_space=pltpu.HBM)],
        out_shape=[jax.ShapeDtypeStruct((part * width, d), F32), pltpu.HBM((part * width, rows), BF)],
        scratch_shapes=[
            pltpu.VMEM((part, rows), jnp.int32),
            pltpu.VMEM((part, width, size), BF),
            pltpu.VMEM((rows, d), BF),
            pltpu.VMEM((part * width, rows), BF),
            pltpu.SemaphoreType.DMA((4,)),
        ],
        compiler_params=pltpu.CompilerParams(vmem_limit_bytes=24 * MIB),
        name="cross_first",
    )(half, codes_t, books_t, corpus)


def dist_kernel(half_ref, rot_hbm, corpus_hbm, words_hbm, out_ref, rot, corpus, words, sems):
    cols = words.shape[0]
    first = pl.multiple_of(half_ref[0] * cols, cols)
    loads = [
        pltpu.make_async_copy(corpus_hbm, corpus, sems.at[0]),
        pltpu.make_async_copy(rot_hbm.at[:, pl.ds(first, cols)], rot, sems.at[1]),
        pltpu.make_async_copy(words_hbm, words, sems.at[2]),
    ]
    for load in loads:
        load.start()
    for load in loads:
        load.wait()
    rotated = lax.dot_general(rot[...], corpus[...], (((0,), (1,)), ((), ())), preferred_element_type=F32)
    gap = rotated - words[...].astype(F32)
    out_ref[...] = jnp.sum(gap * gap, axis=0, keepdims=True)


def distortion(half, rotation, corpus, words):
    rows, d = corpus.shape
    cols = words.shape[0]
    return pl.pallas_call(
        dist_kernel,
        in_specs=[pl.BlockSpec(memory_space=pltpu.SMEM)] + [pl.BlockSpec(memory_space=pl.ANY)] * 3,
        out_specs=pl.BlockSpec(memory_space=pltpu.VMEM),
        out_shape=jax.ShapeDtypeStruct((1, rows), F32),
        scratch_shapes=[
            pltpu.VMEM((d, cols), BF),
            pltpu.VMEM((rows, d), BF),
            pltpu.VMEM((cols, rows), BF),
            pltpu.SemaphoreType.DMA((3,)),
        ],
        compiler_params=pltpu.CompilerParams(vmem_limit_bytes=24 * MIB),
        name="distortion",
    )(half, rotation, corpus, words)


def polar_polynomial(steps):
    poly = np.polynomial.polynomial
    e, out = np.array([0.0, 1.0]), np.array([1.0])
    for _ in range(steps):
        out = poly.polymul(out, poly.polyadd([1.0], 0.5 * e))
        sq = poly.polymul(e, e)
        e = poly.polyadd(0.75 * sq, 0.25 * poly.polymul(sq, e))
    return [float(v) for v in out]


def put(hi, lo, i, first, val):
    r = slice(i * BLK, (i + 1) * BLK)
    last = first + val.shape[1]
    hi[r, first:last], lo[r, first:last] = split(val)
    begin = max(first, (i + 1) * BLK)
    if begin < last:
        hi[begin:last, r], lo[begin:last, r] = split(val[:, begin - first:].T)


def gram(hi, lo, i, first, last):
    r, c = slice(i * BLK, (i + 1) * BLK), slice(first, last)
    return nt(hi[r, :], hi[c, :]) + (nt(hi[r, :], lo[c, :]) + nt(lo[r, :], hi[c, :]))


def square(hi, lo, i):
    r, c = slice(i * BLK, (i + 1) * BLK), slice(i * BLK, hi.shape[0])
    return nn(hi[r, :], hi[:, c]) + (nn(hi[r, :], lo[:, c]) + nn(lo[r, :], hi[:, c]))


def thin(u, hi, lo):
    h, l = split(u)
    m = u.shape[0]
    p = nn(jnp.concatenate([h, l], axis=0), hi[...])
    return p[:m] + (p[m:] + nn(h, lo[...]))


def polar_kernel(coef, place_ref, own_ref, oth_hbm, out_ref, oth, yh, yl, gh, gl, bh, bl, gf, bf, turned, sem):
    n = yh.shape[0]
    half = n // 2
    blocks = n // BLK
    rows = out_ref.shape[0]
    load = pltpu.make_async_copy(oth_hbm, oth, sem)
    load.start()
    col = pl.multiple_of(place_ref[1] * 128, 128)
    yh[:half, :], yl[:half, :] = split(own_ref[...])
    turned[:, :half] = own_ref[:, pl.ds(col, 128)].T
    total = jnp.zeros((), F32)
    for i in range(half // BLK):
        g = gram(yh, yl, i, i * BLK, half)
        gf[i * BLK:(i + 1) * BLK, i * BLK:half] = g
        put(gh, gl, i, i * BLK, g)
        sq = g * g
        total = total + 2.0 * jnp.sum(sq) - jnp.sum(sq[:, :BLK])
    load.wait()
    yh[half:, :], yl[half:, :] = split(oth[...])
    turned[:, half:] = oth[:, pl.ds(col, 128)].T
    for i in range(blocks):
        first = max(half, i * BLK)
        g = gram(yh, yl, i, first, n)
        gf[i * BLK:(i + 1) * BLK, first:] = g
        put(gh, gl, i, first, g)
        sq = g * g
        total = total + 2.0 * jnp.sum(sq)
        if i * BLK >= half:
            total = total - jnp.sum(sq[:, :BLK])
    root = lax.rsqrt(jnp.full((8, 128), total + 1e-06, F32))
    f2 = jnp.max(root)
    f1 = jnp.max(jnp.sqrt(root))
    for i in range(blocks):
        at = slice(i * BLK, (i + 1) * BLK), slice(i * BLK, n)
        b = (2.0 * f2) * gf[at] - (f2 * f2) * square(gh, gl, i)
        bf[at] = b
        put(bh, bl, i, i * BLK, b)
    for i in range(blocks):
        at = slice(i * BLK, (i + 1) * BLK), slice(i * BLK, n)
        put(yh, yl, i, i * BLK, 2.0 * bf[at] - square(bh, bl, i))

    first = turned[pl.ds(pl.multiple_of(place_ref[2] * rows, rows), rows), :] * f1
    pair = jnp.concatenate([first, first - f2 * thin(first, gh, gl)], axis=0)
    quad = jnp.concatenate([pair, pair - thin(pair, bh, bl)], axis=0)

    def mix(k):
        terms = [coef[4 * k + q] * quad[q * rows:(q + 1) * rows] for q in range(4) if 4 * k + q < len(coef)]
        return functools.reduce(lambda a, b: a + b, terms)

    u = mix((len(coef) - 1) // 4)
    for k in range((len(coef) - 1) // 4 - 1, -1, -1):
        u = u - thin(u, yh, yl) + mix(k)
    u = u * math.sqrt(n)
    low = place_ref[0] == 0
    out_ref[:, :half] = jnp.where(low, u[:, :half], u[:, half:])
    out_ref[:, half:] = jnp.where(low, u[:, half:], u[:, :half])


def polar(place, own, oth):
    half, n = own.shape
    part, full = pltpu.VMEM((n, n), BF), pltpu.VMEM((n, n), F32)
    return pl.pallas_call(
        functools.partial(polar_kernel, polar_polynomial(ITERS)),
        in_specs=[
            pl.BlockSpec(memory_space=pltpu.SMEM),
            pl.BlockSpec(memory_space=pltpu.VMEM),
            pl.BlockSpec(memory_space=pl.ANY),
        ],
        out_specs=pl.BlockSpec(memory_space=pltpu.VMEM),
        out_shape=jax.ShapeDtypeStruct((32, n), F32),
        scratch_shapes=[pltpu.VMEM((half, n), F32)] + [part] * 6 + [full] * 2
        + [pltpu.VMEM((128, n), F32), pltpu.SemaphoreType.DMA],
        compiler_params=pltpu.CompilerParams(vmem_limit_bytes=40 * MIB),
        name="polar",
    )(place, own, oth)


AXES = ("gx", "gy")
CORES, SIDE, DEPTH = 2, 4, 8


def place_of(y, x, c, z):
    return ((y * SIDE + x) * CORES + c) * DEPTH + z


def ring_pairs(n, odd):
    pairs = [((i + odd) % n, (i + 1 + odd) % n) for i in range(0, n, 2)]
    return [p if k % 2 == 0 else p[::-1] for k, p in enumerate(pairs)]


def cube_groups():
    return [
        [place_of(y, x, c, z) for y in py for x in px for z in pz]
        for c in range(CORES)
        for py in ring_pairs(SIDE, c)
        for px in ring_pairs(SIDE, c)
        for pz in ring_pairs(DEPTH, c)
    ]


def square_groups():
    return [
        [place_of(y, x, c, z) for y in py for x in px]
        for c in range(CORES)
        for py in ring_pairs(SIDE, 1 - c)
        for px in ring_pairs(SIDE, 1 - c)
        for z in range(DEPTH)
    ]


def swap(fn):
    return [
        (place_of(y, x, c, z), place_of(*fn(y, x, c, z)))
        for y in range(SIDE) for x in range(SIDE) for c in range(CORES) for z in range(DEPTH)
    ]


def mate(n, odd):
    table = {}
    for i in range(0, n, 2):
        a, b = (i + odd) % n, (i + 1 + odd) % n
        table[a], table[b] = b, a
    return table


def far(c):
    table = {}
    for a, b in ((0, 3), (4, 7), (2, 5), (6, 1)):
        a, b = (a + c) % DEPTH, (b + c) % DEPTH
        table[a], table[b] = b, a
    return table


SWAP_CORE = swap(lambda y, x, c, z: (y, x, 1 - c, z))
SWAP_Z = swap(lambda y, x, c, z: (y, x, c, mate(DEPTH, 1 - c)[z]))
SWAP_FAR = swap(lambda y, x, c, z: (y, x, c, far(c)[z]))


def send(value, pairs):
    return lax.ppermute(value, AXES, pairs)


def reduce_half(value, bit, pairs):
    half = value.shape[0] // 2
    away = lax.dynamic_slice_in_dim(value, (1 - bit) * half, half, 0)
    keep = lax.dynamic_slice_in_dim(value, bit * half, half, 0)
    return keep + send(away, pairs)


def gather_half(value, bit, pairs):
    other = send(value, pairs)
    return jnp.where(bit == 0, jnp.concatenate([value, other]), jnp.concatenate([other, value]))


def body(corpus, rotation, code_table, codebooks):
    rows, d = corpus.shape
    gx = lax.axis_index("gx")
    core = gx % CORES
    codes_t = code_table.T
    books_t = codebooks.transpose(0, 2, 1)
    held = [pltpu.with_memory_space_constraint(v, pltpu.HBM) for v in (codes_t, books_t, corpus, rotation)]
    scale = 1.0 / math.sqrt(rows * lax.axis_size("gx") * lax.axis_size("gy"))

    far_half, near_half = (1 - core).reshape(1), core.reshape(1)
    far_term, far_words = cross_first(far_half, held[0], held[1], held[2], scale)
    arrived = send(far_term, SWAP_CORE)
    near_term, near_words = cross_first(near_half, held[0], held[1], held[2], scale)

    groups = cube_groups()
    members = len(groups[0])
    summed = (near_term + arrived).reshape(members, -1, d)
    pieces = lax.all_to_all(summed, AXES, 0, 0, axis_index_groups=groups)
    piece = jnp.sum(pieces, axis=0)

    inner = square_groups()
    parts = lax.all_to_all(piece.reshape(len(inner[0]), -1, d), AXES, 0, 0, axis_index_groups=inner)
    part = jnp.sum(parts, axis=0)
    part = part + send(part, SWAP_Z)
    part, far_words = lax.optimization_barrier((part, far_words))
    other = send(part, SWAP_FAR)
    gaps = distortion(far_half, held[3], held[2], far_words)
    other, gaps = lax.optimization_barrier((other, gaps))
    part = part + other
    parts = lax.all_to_all(jnp.broadcast_to(part[None], parts.shape), AXES, 0, 0, axis_index_groups=inner)
    piece = parts.reshape(-1, d)
    own = lax.all_to_all(jnp.broadcast_to(piece[None], (members,) + piece.shape), AXES, 0, 0, axis_index_groups=groups)
    own = own.reshape(-1, d)
    own, near_words = lax.optimization_barrier((own, near_words))
    other = send(own, SWAP_CORE)
    gaps = gaps + distortion(near_half, held[3], held[2], near_words)
    other, gaps = lax.optimization_barrier((other, gaps))
    place = jnp.stack([core, gx // 4, gx % 4])
    return polar(place, own, other), gaps.reshape(rows)


def solution(mesh):
    return jax.shard_map(
        body,
        mesh=mesh,
        in_specs=(P(("gx", "gy"), None), P(), P(("gx", "gy"), None), P()),
        out_specs=(P("gx", None), P(("gx", "gy"))),
        check_vma=False,
    )
```

time: 136 us -> 120 us (0.88)
  blocking collectives: 22.4 us -> 64.8 us
  waiting for transfers between devices: 43 us -> 6.36 us
  starting transfers between devices: 17.6 us -> 6.63 us
  local copies, waits for them, and re-layouts: 5.99 us -> 0.27 us
  other arithmetic: 5.14 us -> 1.3 us
  Pallas kernels: 40.6 us -> 39.2 us
    all_to_all x0 -> x3, blocking collectives: none -> 42.9 us  [the longest x1 28.8 us: body(): pieces = lax.all_to_all(summed, AXES, 0, 0, axis_index_groups=groups)]
    all_to_all x1 -> x0, waiting for transfers between devices: 19.5 us -> none  [body(): pieces = lax.all_to_all(summed, AXES, 0, 0, axis_index_groups=groups)]
    ppermute x8 -> x4, waiting for transfers between devices: 23.5 us -> 6.36 us  [send(): return lax.ppermute(value, AXES, pairs)]
    all_to_all x1 -> x0, starting transfers between devices: 9.76 us -> none  [body(): pieces = lax.all_to_all(summed, AXES, 0, 0, axis_index_groups=groups)]
    unnamed x20 -> x4, local copies, waits for them, and re-layouts: 5.71 us -> 0.01 us
    reduce_sum x1, other arithmetic: 1.74 us -> 0.14 us  [body(): piece = jnp.sum(pieces, axis=0)]
    pallas_call x5, Pallas kernels: 40.6 us -> 39.2 us  [the longest x1 23.6 us: polar(): pl.pallas_call(functools.partial(polar_kernel, polar_polynomial(ITERS)),...]
    ppermute x8 -> x4, starting transfers between devices: 7.84 us -> 6.63 us  [send(): return lax.ppermute(value, AXES, pairs)]
  transfers between devices with their start and end apart: 9 -> 4, of which waited for: 8 -> 2; matrix products, arithmetic and copies ran while one was open for 0% -> 1% of each run, Pallas kernels for 5% -> 9%
where the time goes in v2:
time: 120 us; the launch traced here: 119 us
  blocking collectives  64.8 us (54%)
  Pallas kernels  39.2 us (33%)
  starting transfers between devices  6.63 us (6%)
  waiting for transfers between devices  6.36 us (5%)
  other arithmetic  1.3 us (1%)
    all_to_all x1, blocking collectives, body(): pieces = lax.all_to_all(summed, AXES, 0, 0, axis_index_groups=groups)  28.8 us
    pallas_call x1, Pallas kernels, polar(): pl.pallas_call(functools.partial(polar_kernel, polar_polynomial(ITERS)),...  23.6 us
    all_to_all x1, blocking collectives, body(): lax.all_to_all(jnp.broadcast_to(piece[None], (members,) + piece.shape), A...  21.9 us
    pallas_call x2, Pallas kernels, cross_first(): pl.pallas_call(functools.partial(first_kernel, scale), in_specs=[pl.Block...  9.23 us
    all_to_all x1, blocking collectives, body(): lax.all_to_all(piece.reshape(len(inner[0]), -1, d), AXES, 0, 0, axis_inde...  7.09 us
    all_to_all x1, blocking collectives, body(): lax.all_to_all(jnp.broadcast_to(part[None], parts.shape), AXES, 0, 0, axi...  6.97 us
    ppermute x4, starting transfers between devices, send(): return lax.ppermute(value, AXES, pairs)  6.63 us
    pallas_call x2, Pallas kernels, distortion(): pl.pallas_call(dist_kernel, in_specs=[pl.BlockSpec(memory_space=pltpu.SME...  6.37 us
  transfers between devices with their start and end apart: 4, of which 2 were waited for; matrix products, arithmetic and copies ran while one was open for 1% of the time, Pallas kernels for 9%

profile of v2, /device:TPU:1, one launch (start us, length us, event | category | flops | bytes accessed | tf_op | source)
XLA Modules:
  0.0 119.4 jit_solution(1985476836916796315)
XLA Ops:
  0.6 4.6 %cross_first.3 = (f32[512,1024]{1,0:T(8,128)S(1)}, bf16[512,1024]{1,0:T(8,128)(2,1)}) custom-call(s32[1]{0:T(128)} %bitcast.5.half_ref, s32[64,1024]{1,0:T(8,128)} %bitcast.16, bf16[64,16,256]{2,1,0:T(8,128)(2,1)} %bitcast.14, bf16[1024,1024]{1,0:T(8,128)(2,1)} %corpus_hbm.7), custom_call_target="tpu_custom_call" | custom-call | tf_op jit(solution)/shard_map/cross_first/pallas_call | solution.py:64
  5.3 3.3 %collective-permute-start = (f32[512,1024]{1,0:T(8,128)S(1)}, f32[512,1024]{1,0:T(8,128)S(1)}, u32[]{:S(2)}, u32[]{:S(2)}) collective-permute-start(f32[512,1024]{1,0:T(8,128)S(1)} %get-tuple-element.15), channel_id=1, source_target_pairs={{0,8},{1,9},{2,10},{3,11},{4,12},{5,13},{6,14},{7,15},{8,0},{9,1},... | collective-permute-start | bytes 6291464 | tf_op jit(solution)/shard_map/ppermute | solution.py:292
  8.6 4.6 %cross_first.2 = (f32[512,1024]{1,0:T(8,128)S(1)}, bf16[512,1024]{1,0:T(8,128)(2,1)}) custom-call(s32[1]{0:T(128)} %bitcast.half_ref, s32[64,1024]{1,0:T(8,128)} %bitcast.17, bf16[64,16,256]{2,1,0:T(8,128)(2,1)} %bitcast.15, bf16[1024,1024]{1,0:T(8,128)(2,1)} %corpus_hbm.7), custom_call_target="tpu_custom_call" | custom-call | tf_op jit(solution)/shard_map/cross_first/pallas_call | solution.py:64
  13.2 0.0 collective-permute-done
  13.2 0.5 add.22
  13.7 28.8 %all_to_all.20 = f32[8,64,1024]{2,1,0:T(8,128)S(1)} all-to-all(f32[8,64,1024]{2,1,0:T(8,128)S(1)} %bitcast.13), channel_id=1, replica_groups={{0,1,16,17,64,65,80,81},{3,2,19,18,67,66,83,82},{4,5,20,21,68,69,84,85}..., dimensions={0} | all-to-all | bytes 4194304 | tf_op jit(solution)/shard_map/all_to_all | solution.py:324
  42.5 0.1 reduce_sum.18
  42.7 7.1 %all_to_all.21 = f32[4,16,1024]{2,1,0:T(8,128)S(1)} all-to-all(f32[4,16,1024]{2,1,0:T(8,128)S(1)} %bitcast.18), channel_id=1, replica_groups={{80,96,144,160},{81,97,145,161},{82,98,146,162},{83,99,147,163},{84,100..., dimensions={0} | all-to-all | bytes 524288 | tf_op jit(solution)/shard_map/all_to_all | solution.py:328
  49.8 0.1 collective-permute-start.1
  49.9 3.4 %collective-permute-done.1 = f32[16,1024]{1,0:T(8,128)S(1)} collective-permute-done((f32[16,1024]{1,0:T(8,128)S(1)}, f32[16,1024]{1,0:T(8,128)S(1)}, u32[]{:S(2)}, u32[]{:S(2)}) %collective-permute-start.1) | collective-permute-done | bytes 65568 | tf_op jit(solution)/shard_map/ppermute | solution.py:292
  53.3 0.5 collective-permute-start.2
  53.8 0.0 copy-done.1
  53.8 3.2 %distortion.2 = f32[1,1024]{1,0:T(1,128)S(1)} custom-call(s32[1]{0:T(128)} %bitcast.5.half_ref, bf16[1024,1024]{1,0:T(8,128)(2,1)} %rot_hbm.3, bf16[1024,1024]{1,0:T(8,128)(2,1)} %corpus_hbm.7, bf16[512,1024]{1,0:T(8,128)(2,1)S(1)} %copy-done.1), custom_call_target="tpu_custom_call" | custom-call | tf_op jit(solution)/shard_map/distortion/pallas_call | solution.py:101
  57.0 2.9 %collective-permute-done.2 = f32[16,1024]{1,0:T(8,128)S(1)} collective-permute-done((f32[16,1024]{1,0:T(8,128)S(1)}, f32[16,1024]{1,0:T(8,128)S(1)}, u32[]{:S(2)}, u32[]{:S(2)}) %collective-permute-start.2) | collective-permute-done | bytes 65568 | tf_op jit(solution)/shard_map/ppermute | solution.py:292
  60.0 7.0 %all_to_all.22 = f32[4,16,1024]{2,1,0:T(8,128)S(1)} all-to-all(f32[4,16,1024]{2,1,0:T(8,128)S(1)} %broadcast_in_dim.6), channel_id=1, replica_groups={{80,96,144,160},{81,97,145,161},{82,98,146,162},{83,99,147,163},{84,100..., dimensions={0} | all-to-all | bytes 524288 | tf_op jit(solution)/shard_map/all_to_all | solution.py:336
  66.9 0.2 broadcast_in_dim.15
  67.2 0.0 copy-start
  67.2 21.9 %all_to_all.23 = f32[8,64,1024]{2,1,0:T(8,128)S(1)} all-to-all(f32[8,64,1024]{2,1,0:T(8,128)S(1)} %broadcast_in_dim.15), channel_id=1, replica_groups={{0,1,16,17,64,65,80,81},{3,2,19,18,67,66,83,82},{4,5,20,21,68,69,84,85}..., dimensions={0} | all-to-all | bytes 4194304 | tf_op jit(solution)/shard_map/all_to_all | solution.py:338
  89.1 2.7 %collective-permute-start.3 = (f32[512,1024]{1,0:T(8,128)S(1)}, f32[512,1024]{1,0:T(8,128)}, u32[]{:S(2)}, u32[]{:S(2)}) collective-permute-start(f32[512,1024]{1,0:T(8,128)S(1)} %bitcast.11), channel_id=1, source_target_pairs={{0,8},{1,9},{2,10},{3,11},{4,12},{5,13},{6,14},{7,15},{8,0},{9,1},... | collective-permute-start | bytes 6291464 | tf_op jit(solution)/shard_map/ppermute | solution.py:292
  91.7 0.1 pad_add_fusion.place_ref
  91.8 3.2 %distortion.3 = f32[1,1024]{1,0:T(1,128)S(1)} custom-call(s32[1]{0:T(128)} %bitcast.half_ref, bf16[1024,1024]{1,0:T(8,128)(2,1)} %rot_hbm.3, bf16[1024,1024]{1,0:T(8,128)(2,1)} %corpus_hbm.7, bf16[512,1024]{1,0:T(8,128)(2,1)S(1)} %copy-done), custom_call_target="tpu_custom_call" | custom-call | tf_op jit(solution)/shard_map/distortion/pallas_call | solution.py:101
  95.0 0.6 add.25
  95.6 0.0 collective-permute-done.3.oth_hbm
  95.7 23.6 %polar.1 = f32[32,1024]{1,0:T(8,128)} custom-call(s32[3]{0:T(128)S(1)} %pad_add_fusion.place_ref, f32[512,1024]{1,0:T(8,128)S(1)} %bitcast.12, f32[512,1024]{1,0:T(8,128)} %collective-permute-done.3.oth_hbm), custom_call_target="tpu_custom_call" | custom-call | tf_op jit(solution)/shard_map/polar/pallas_call | solution.py:214
  (6 shorter events, 0.1 us)
Async XLA Ops:
  5.3 7.9 %collective-permute-start = (f32[512,1024]{1,0:T(8,128)S(1)}, f32[512,1024]{1,0:T(8,128)S(1)}, u32[]{:S(2)}, u32[]{:S(2)}) collective-permute-start(f32[512,1024]{1,0:T(8,128)S(1)} %get-tuple-element.15), channel_id=1, source_target_pairs={{0,8},{1,9},{2,10},{3,11},{4,12},{5,13},{6,14},{7,15},{8,0},{9,1},... | collective-permute-start | bytes 6291464 | tf_op jit(solution)/shard_map/ppermute | solution.py:292
  42.5 11.3 %copy-start.1 = (bf16[512,1024]{1,0:T(8,128)(2,1)S(1)}, bf16[512,1024]{1,0:T(8,128)(2,1)}, u32[]{:S(2)}) copy-start(bf16[512,1024]{1,0:T(8,128)(2,1)} %get-tuple-element.18.words_hbm) | copy-start | bytes 3145732
  49.8 3.5 %collective-permute-start.1 = (f32[16,1024]{1,0:T(8,128)S(1)}, f32[16,1024]{1,0:T(8,128)S(1)}, u32[]{:S(2)}, u32[]{:S(2)}) collective-permute-start(f32[16,1024]{1,0:T(8,128)S(1)} %reduce_sum.19), channel_id=1, source_target_pairs={{0,7},{1,2},{2,1},{3,4},{4,3},{5,6},{6,5},{7,0},{8,9},{9,8},{10,11... | collective-permute-start | bytes 196616 | tf_op jit(solution)/shard_map/ppermute | solution.py:292
  53.3 6.6 %collective-permute-start.2 = (f32[16,1024]{1,0:T(8,128)S(1)}, f32[16,1024]{1,0:T(8,128)S(1)}, u32[]{:S(2)}, u32[]{:S(2)}) collective-permute-start(f32[16,1024]{1,0:T(8,128)S(1)} %add.23), channel_id=1, source_target_pairs={{0,3},{1,6},{2,5},{3,0},{4,7},{5,2},{6,1},{7,4},{8,13},{9,12},{10,... | collective-permute-start | bytes 196616 | tf_op jit(solution)/shard_map/ppermute | solution.py:292
  67.2 24.6 %copy-start = (bf16[512,1024]{1,0:T(8,128)(2,1)S(1)}, bf16[512,1024]{1,0:T(8,128)(2,1)}, u32[]{:S(2)}) copy-start(bf16[512,1024]{1,0:T(8,128)(2,1)} %get-tuple-element.23.words_hbm) | copy-start | bytes 3145732
  89.1 6.6 %collective-permute-start.3 = (f32[512,1024]{1,0:T(8,128)S(1)}, f32[512,1024]{1,0:T(8,128)}, u32[]{:S(2)}, u32[]{:S(2)}) collective-permute-start(f32[512,1024]{1,0:T(8,128)S(1)} %bitcast.11), channel_id=1, source_target_pairs={{0,8},{1,9},{2,10},{3,11},{4,12},{5,13},{6,14},{7,15},{8,0},{9,1},... | collective-permute-start | bytes 6291464 | tf_op jit(solution)/shard_map/ppermute | solution.py:292

commit v3 on v2

--- a/solution.py
+++ b/solution.py
@@ -22,48 +22,48 @@
 def nn(a, b):
     return lax.dot_general(a, b, (((1,), (0,)), ((), ())), preferred_element_type=F32)
 
-def rebuild(codes, books, words, row, word_at):
-    subs = words.shape[0] // books.shape[1]
+def rebuild(codes, books, words, block):
     width = books.shape[1]
     word = lax.broadcasted_iota(jnp.int16, (books.shape[2], codes.shape[1]), 0)
     one, zero = jnp.ones((), BF), jnp.zeros((), BF)
-    for block in range(subs // CHUNK):
-        picks = codes[pl.ds(row + block * CHUNK, CHUNK), :].astype(jnp.int16)
-        for k in range(CHUNK):
-            s = block * CHUNK + k
-            hot = jnp.where(word == picks[k:k + 1, :], one, zero)
-            words[s * width:(s + 1) * width, :] = nn(books[word_at + s], hot).astype(BF)
-
-
-def first_kernel(scale, half_ref, codes_hbm, books_hbm, corpus_hbm, out, words_hbm, codes, books, corpus, words, sems):
+    picks = codes[block * CHUNK:(block + 1) * CHUNK, :].astype(jnp.int16)
+    for k in range(CHUNK):
+        s = block * CHUNK + k
+        hot = jnp.where(word == picks[k:k + 1, :], one, zero)
+        words[s * width:(s + 1) * width, :] = nn(books[s], hot).astype(BF)
+
+
+def first_kernel(scale, half_ref, mine_ref, codes_hbm, books_hbm, corpus_hbm, out, words_hbm, codes, books, corpus, words, sems):
     subs = books.shape[0]
     first = pl.multiple_of(half_ref[0] * subs, subs)
-    loads = [
-        pltpu.make_async_copy(codes_hbm.at[pl.ds(first, subs)], codes, sems.at[0]),
-        pltpu.make_async_copy(books_hbm.at[pl.ds(first, subs)], books, sems.at[1]),
-        pltpu.make_async_copy(corpus_hbm, corpus, sems.at[2]),
-    ]
-    for load in loads:
+    tables = []
+    for block in range(subs // CHUNK):
+        at, to = pl.ds(first + block * CHUNK, CHUNK), pl.ds(block * CHUNK, CHUNK)
+        tables.append(pltpu.make_async_copy(codes_hbm.at[at], codes.at[to], sems.at[2 * block]))
+        tables.append(pltpu.make_async_copy(books_hbm.at[at], books.at[to], sems.at[2 * block + 1]))
+    whole = pltpu.make_async_copy(corpus_hbm, corpus, sems.at[len(tables)])
+    for load in tables + [whole]:
         load.start()
-    loads[0].wait()
-    loads[1].wait()
-    rebuild(codes, books, words, 0, 0)
-    stores = [pltpu.make_async_copy(words, words_hbm, sems.at[3])]
-    stores[0].start()
-    loads[2].wait()
+    for block in range(subs // CHUNK):
+        tables[2 * block].wait()
+        tables[2 * block + 1].wait()
+        rebuild(codes, books, words, block)
+    store = pltpu.make_async_copy(words, words_hbm, sems.at[len(tables) + 1])
+    store.start()
+    whole.wait()
     for k in range(corpus.shape[1] // BLK):
         c = slice(k * BLK, (k + 1) * BLK)
         out[:, c] = nn(words[...], corpus[:, c]) * scale
-    stores[0].wait()
-
-
-def cross_first(half, codes_t, books_t, corpus, scale):
+    store.wait()
+
+
+def cross_half(half, mine, codes_t, books_t, corpus, scale):
     subs, width, size = books_t.shape
     rows, d = corpus.shape
     part = subs // 2
     return pl.pallas_call(
         functools.partial(first_kernel, scale),
-        in_specs=[pl.BlockSpec(memory_space=pltpu.SMEM)] + [pl.BlockSpec(memory_space=pl.ANY)] * 3,
+        in_specs=[pl.BlockSpec(memory_space=pltpu.SMEM)] * 2 + [pl.BlockSpec(memory_space=pl.ANY)] * 3,
         out_specs=[pl.BlockSpec(memory_space=pltpu.VMEM), pl.BlockSpec(memory_space=pltpu.HBM)],
         out_shape=[jax.ShapeDtypeStruct((part * width, d), F32), pltpu.HBM((part * width, rows), BF)],
         scratch_shapes=[
@@ -71,14 +71,57 @@
             pltpu.VMEM((part, width, size), BF),
             pltpu.VMEM((rows, d), BF),
             pltpu.VMEM((part * width, rows), BF),
-            pltpu.SemaphoreType.DMA((4,)),
+            pltpu.SemaphoreType.DMA((2 + 2 * (part // CHUNK),)),
         ],
         compiler_params=pltpu.CompilerParams(vmem_limit_bytes=24 * MIB),
-        name="cross_first",
-    )(half, codes_t, books_t, corpus)
-
-
-def dist_kernel(half_ref, rot_hbm, corpus_hbm, words_hbm, out_ref, rot, corpus, words, sems):
+        name="cross_half",
+    )(half, mine, codes_t, books_t, corpus)
+
+
+def pick_kernel(mine_ref, pieces_ref, *out_refs):
+    rows = out_refs[0].shape[0]
+    for k, out_ref in enumerate(out_refs):
+        at = pl.ds(pl.multiple_of((mine_ref[0] ^ k) * rows, rows), rows)
+        total = pieces_ref[0, at, :]
+        for p in range(1, pieces_ref.shape[0]):
+            total = total + pieces_ref[p, at, :]
+        out_ref[...] = total
+
+
+def pick(mine, pieces):
+    _, rows, d = pieces.shape
+    return pl.pallas_call(
+        pick_kernel,
+        in_specs=[pl.BlockSpec(memory_space=pltpu.SMEM), pl.BlockSpec(memory_space=pltpu.VMEM)],
+        out_specs=[pl.BlockSpec(memory_space=pltpu.VMEM)] * 4,
+        out_shape=[jax.ShapeDtypeStruct((rows // 4, d), F32)] * 4,
+        compiler_params=pltpu.CompilerParams(vmem_limit_bytes=8 * MIB),
+        name="pick",
+    )(mine, pieces)
+
+
+def spread_kernel(mine_ref, *refs):
+    *part_refs, out_ref = refs
+    rows = part_refs[0].shape[0]
+    for k, part_ref in enumerate(part_refs):
+        at = pl.ds(pl.multiple_of((mine_ref[0] ^ k) * rows, rows), rows)
+        for p in range(out_ref.shape[0]):
+            out_ref[p, at, :] = part_ref[...]
+
+
+def spread(mine, parts, members):
+    rows, d = parts[0].shape
+    return pl.pallas_call(
+        spread_kernel,
+        in_specs=[pl.BlockSpec(memory_space=pltpu.SMEM)] + [pl.BlockSpec(memory_space=pltpu.VMEM)] * 4,
+        out_specs=pl.BlockSpec(memory_space=pltpu.VMEM),
+        out_shape=jax.ShapeDtypeStruct((members, 4 * rows, d), F32),
+        compiler_params=pltpu.CompilerParams(vmem_limit_bytes=8 * MIB),
+        name="spread",
+    )(mine, *parts)
+
+
+def dist_kernel(half_ref, sums_ref, rot_hbm, corpus_hbm, words_hbm, out_ref, rot, corpus, words, sems):
     cols = words.shape[0]
     first = pl.multiple_of(half_ref[0] * cols, cols)
     loads = [
@@ -92,15 +135,15 @@
         load.wait()
     rotated = lax.dot_general(rot[...], corpus[...], (((0,), (1,)), ((), ())), preferred_element_type=F32)
     gap = rotated - words[...].astype(F32)
-    out_ref[...] = jnp.sum(gap * gap, axis=0, keepdims=True)
-
-
-def distortion(half, rotation, corpus, words):
+    out_ref[...] = sums_ref[...] + jnp.sum(gap * gap, axis=0, keepdims=True)
+
+
+def distortion(half, sums, rotation, corpus, words):
     rows, d = corpus.shape
     cols = words.shape[0]
     return pl.pallas_call(
         dist_kernel,
-        in_specs=[pl.BlockSpec(memory_space=pltpu.SMEM)] + [pl.BlockSpec(memory_space=pl.ANY)] * 3,
+        in_specs=[pl.BlockSpec(memory_space=pltpu.SMEM), pl.BlockSpec(memory_space=pltpu.VMEM)] + [pl.BlockSpec(memory_space=pl.ANY)] * 3,
         out_specs=pl.BlockSpec(memory_space=pltpu.VMEM),
         out_shape=jax.ShapeDtypeStruct((1, rows), F32),
         scratch_shapes=[
@@ -111,7 +154,7 @@
         ],
         compiler_params=pltpu.CompilerParams(vmem_limit_bytes=24 * MIB),
         name="distortion",
-    )(half, rotation, corpus, words)
+    )(half, sums, rotation, corpus, words)
 
 
 def polar_polynomial(steps):
@@ -133,14 +176,23 @@
         hi[begin:last, r], lo[begin:last, r] = split(val[:, begin - first:].T)
 
 
-def gram(hi, lo, i, first, last):
+def inner(hi, lo, i, first, last, mul):
     r, c = slice(i * BLK, (i + 1) * BLK), slice(first, last)
-    return nt(hi[r, :], hi[c, :]) + (nt(hi[r, :], lo[c, :]) + nt(lo[r, :], hi[c, :]))
-
-
-def square(hi, lo, i):
-    r, c = slice(i * BLK, (i + 1) * BLK), slice(i * BLK, hi.shape[0])
-    return nn(hi[r, :], hi[:, c]) + (nn(hi[r, :], lo[:, c]) + nn(lo[r, :], hi[:, c]))
+
+    def times(a, b, at):
+        return mul(a[r, :], b[at, :] if mul is nt else b[:, at])
+
+    mixed = times(hi, lo, c)
+    if first > i * BLK:
+        mixed = mixed + times(lo, hi, c)
+    else:
+        corner = mixed[:, :BLK] + mixed[:, :BLK].T
+        if last > first + BLK:
+            rest = mixed[:, BLK:] + times(lo, hi, slice(first + BLK, last))
+            mixed = jnp.concatenate([corner, rest], axis=1)
+        else:
+            mixed = corner
+    return times(hi, hi, c) + mixed
 
 
 def thin(u, hi, lo):
@@ -162,7 +214,7 @@
     turned[:, :half] = own_ref[:, pl.ds(col, 128)].T
     total = jnp.zeros((), F32)
     for i in range(half // BLK):
-        g = gram(yh, yl, i, i * BLK, half)
+        g = inner(yh, yl, i, i * BLK, half, nt)
         gf[i * BLK:(i + 1) * BLK, i * BLK:half] = g
         put(gh, gl, i, i * BLK, g)
         sq = g * g
@@ -172,7 +224,7 @@
     turned[:, half:] = oth[:, pl.ds(col, 128)].T
     for i in range(blocks):
         first = max(half, i * BLK)
-        g = gram(yh, yl, i, first, n)
+        g = inner(yh, yl, i, first, n, nt)
         gf[i * BLK:(i + 1) * BLK, first:] = g
         put(gh, gl, i, first, g)
         sq = g * g
@@ -184,12 +236,12 @@
     f1 = jnp.max(jnp.sqrt(root))
     for i in range(blocks):
         at = slice(i * BLK, (i + 1) * BLK), slice(i * BLK, n)
-        b = (2.0 * f2) * gf[at] - (f2 * f2) * square(gh, gl, i)
+        b = (2.0 * f2) * gf[at] - (f2 * f2) * inner(gh, gl, i, i * BLK, n, nn)
         bf[at] = b
         put(bh, bl, i, i * BLK, b)
     for i in range(blocks):
         at = slice(i * BLK, (i + 1) * BLK), slice(i * BLK, n)
-        put(yh, yl, i, i * BLK, 2.0 * bf[at] - square(bh, bl, i))
+        put(yh, yl, i, i * BLK, 2.0 * bf[at] - inner(bh, bl, i, i * BLK, n, nn))
 
     first = turned[pl.ds(pl.multiple_of(place_ref[2] * rows, rows), rows), :] * f1
     pair = jnp.concatenate([first, first - f2 * thin(first, gh, gl)], axis=0)
@@ -250,16 +302,6 @@
     ]
 
 
-def square_groups():
-    return [
-        [place_of(y, x, c, z) for y in py for x in px]
-        for c in range(CORES)
-        for py in ring_pairs(SIDE, 1 - c)
-        for px in ring_pairs(SIDE, 1 - c)
-        for z in range(DEPTH)
-    ]
-
-
 def swap(fn):
     return [
         (place_of(y, x, c, z), place_of(*fn(y, x, c, z)))
@@ -287,6 +329,12 @@
 SWAP_Z = swap(lambda y, x, c, z: (y, x, c, mate(DEPTH, 1 - c)[z]))
 SWAP_FAR = swap(lambda y, x, c, z: (y, x, c, far(c)[z]))
 
+SWAP_X = swap(lambda y, x, c, z: (y, mate(SIDE, 1 - c)[x], c, z))
+SWAP_Y = swap(lambda y, x, c, z: (mate(SIDE, 1 - c)[y], x, c, z))
+SWAP_XY = swap(lambda y, x, c, z: (mate(SIDE, 1 - c)[y], mate(SIDE, 1 - c)[x], c, z))
+
+SWAP_BOTH = swap(lambda y, x, c, z: (y, x, c, far(c)[mate(DEPTH, 1 - c)[z]]))
+
 
 def send(value, pairs):
     return lax.ppermute(value, AXES, pairs)
@@ -308,38 +356,36 @@
     rows, d = corpus.shape
     gx = lax.axis_index("gx")
     core = gx % CORES
+    mine = (gx // CORES // SIDE % 2 * 2 + gx // CORES % 2).reshape(1)
     codes_t = code_table.T
     books_t = codebooks.transpose(0, 2, 1)
     held = [pltpu.with_memory_space_constraint(v, pltpu.HBM) for v in (codes_t, books_t, corpus, rotation)]
     scale = 1.0 / math.sqrt(rows * lax.axis_size("gx") * lax.axis_size("gy"))
 
     far_half, near_half = (1 - core).reshape(1), core.reshape(1)
-    far_term, far_words = cross_first(far_half, held[0], held[1], held[2], scale)
+    far_term, far_words = cross_half(far_half, mine, held[0], held[1], held[2], scale)
     arrived = send(far_term, SWAP_CORE)
-    near_term, near_words = cross_first(near_half, held[0], held[1], held[2], scale)
+    near_term, near_words = cross_half(near_half, mine, held[0], held[1], held[2], scale)
 
     groups = cube_groups()
     members = len(groups[0])
     summed = (near_term + arrived).reshape(members, -1, d)
     pieces = lax.all_to_all(summed, AXES, 0, 0, axis_index_groups=groups)
-    piece = jnp.sum(pieces, axis=0)
-
-    inner = square_groups()
-    parts = lax.all_to_all(piece.reshape(len(inner[0]), -1, d), AXES, 0, 0, axis_index_groups=inner)
-    part = jnp.sum(parts, axis=0)
-    part = part + send(part, SWAP_Z)
+    part, *away = pick(mine, pieces)
+    got = [send(v, p) for v, p in zip(away[::-1], (SWAP_XY, SWAP_Y, SWAP_X))]
+    part = part + got[0] + got[1] + got[2]
     part, far_words = lax.optimization_barrier((part, far_words))
-    other = send(part, SWAP_FAR)
-    gaps = distortion(far_half, held[3], held[2], far_words)
-    other, gaps = lax.optimization_barrier((other, gaps))
-    part = part + other
-    parts = lax.all_to_all(jnp.broadcast_to(part[None], parts.shape), AXES, 0, 0, axis_index_groups=inner)
-    piece = parts.reshape(-1, d)
-    own = lax.all_to_all(jnp.broadcast_to(piece[None], (members,) + piece.shape), AXES, 0, 0, axis_index_groups=groups)
+    others = [send(part, pairs) for pairs in (SWAP_BOTH, SWAP_FAR, SWAP_Z)]
+    gaps = distortion(far_half, jnp.zeros((1, rows), F32), held[3], held[2], far_words)
+    others, gaps = lax.optimization_barrier((others, gaps))
+    part = part + others[0] + others[1] + others[2]
+    got = [send(part, p) for p in (SWAP_XY, SWAP_Y, SWAP_X)]
+    gathered = spread(mine, [part] + got[::-1], members)
+    own = lax.all_to_all(gathered, AXES, 0, 0, axis_index_groups=groups)
     own = own.reshape(-1, d)
     own, near_words = lax.optimization_barrier((own, near_words))
     other = send(own, SWAP_CORE)
-    gaps = gaps + distortion(near_half, held[3], held[2], near_words)
+    gaps = distortion(near_half, gaps, held[3], held[2], near_words)
     other, gaps = lax.optimization_barrier((other, gaps))
     place = jnp.stack([core, gx // 4, gx % 4])
     return polar(place, own, other), gaps.reshape(rows)

time: 120 us -> 115 us (0.958)
  blocking collectives: 64.8 us -> 51 us
  starting transfers between devices: 6.63 us -> 18.7 us
  waiting for transfers between devices: 6.36 us -> 4.96 us
    all_to_all x3 -> x1, blocking collectives: 35.9 us -> 22.1 us  [body(): own = lax.all_to_all(gathered, AXES, 0, 0, axis_index_groups=groups)]
    ppermute x4 -> x11, starting transfers between devices: 6.63 us -> 18.7 us  [send(): return lax.ppermute(value, AXES, pairs)]
    pallas_call x1, Pallas kernels: 23.6 us -> 21.8 us  [polar(): pl.pallas_call(functools.partial(polar_kernel, polar_polynomial(ITERS)),...]
    ppermute x4 -> x11, waiting for transfers between devices: 6.36 us -> 4.96 us  [send(): return lax.ppermute(value, AXES, pairs)]
    pallas_call x2 -> x4, Pallas kernels: 9.23 us -> 9.59 us  [the longest x2 9.36 us: cross_half(): pl.pallas_call(functools.partial(first_kernel, scale), in_specs=[pl.Block...]
  transfers between devices with their start and end apart: 4 -> 11, of which waited for: 2 -> 6; matrix products, arithmetic and copies ran while one was open for 1% -> 0% of each run, Pallas kernels for 9% -> 10%
where the time goes in v3:
time: 115 us
  blocking collectives  51 us (44%)
  Pallas kernels  38.4 us (33%)
  starting transfers between devices  18.7 us (16%)
  waiting for transfers between devices  4.96 us (4%)
    all_to_all x1, blocking collectives, body(): pieces = lax.all_to_all(summed, AXES, 0, 0, axis_index_groups=groups)  28.9 us
    all_to_all x1, blocking collectives, body(): own = lax.all_to_all(gathered, AXES, 0, 0, axis_index_groups=groups)  22.1 us
    pallas_call x1, Pallas kernels, polar(): pl.pallas_call(functools.partial(polar_kernel, polar_polynomial(ITERS)),...  21.8 us
    ppermute x11, starting transfers between devices, send(): return lax.ppermute(value, AXES, pairs)  18.7 us
    pallas_call x2, Pallas kernels, cross_half(): pl.pallas_call(functools.partial(first_kernel, scale), in_specs=[pl.Block...  9.36 us
    pallas_call x2, Pallas kernels, distortion(): pl.pallas_call(dist_kernel, in_specs=[pl.BlockSpec(memory_space=pltpu.SME...  6.97 us
    ppermute x11, waiting for transfers between devices, send(): return lax.ppermute(value, AXES, pairs)  4.96 us
  transfers between devices with their start and end apart: 11, of which 6 were waited for; matrix products, arithmetic and copies ran while one was open for 0% of the time, Pallas kernels for 10%

profile of v3, /device:TPU:1, one launch (start us, length us, event | category | flops | bytes accessed | tf_op | source)
XLA Modules:
  0.0 114.7 jit_solution(7901428619783857069)
XLA Ops:
  0.7 4.7 %cross_half.3 = (f32[512,1024]{1,0:T(8,128)S(1)}, bf16[512,1024]{1,0:T(8,128)(2,1)}) custom-call(s32[1]{0:T(128)} %bitcast.6.half_ref, s32[1]{0:T(128)} %bitcast.3.mine_ref, s32[64,1024]{1,0:T(8,128)} %bitcast.15, bf16[64,16,256]{2,1,0:T(8,128)(2,1)} %bitcast.13, bf16[1024,1024]{1,0:T(8,128)(2,1)} %corpus_hbm.7), custom_call_target="tpu_custom_call" | custom-call | tf_op jit(solution)/shard_map/cross_half/pallas_call | solution.py:64
  5.4 3.3 %collective-permute-start = (f32[512,1024]{1,0:T(8,128)S(1)}, f32[512,1024]{1,0:T(8,128)S(1)}, u32[]{:S(2)}, u32[]{:S(2)}) collective-permute-start(f32[512,1024]{1,0:T(8,128)S(1)} %get-tuple-element.21), channel_id=1, source_target_pairs={{0,8},{1,9},{2,10},{3,11},{4,12},{5,13},{6,14},{7,15},{8,0},{9,1},... | collective-permute-start | bytes 6291464 | tf_op jit(solution)/shard_map/ppermute | solution.py:340
  8.7 4.7 %cross_half.2 = (f32[512,1024]{1,0:T(8,128)S(1)}, bf16[512,1024]{1,0:T(8,128)(2,1)}) custom-call(s32[1]{0:T(128)} %bitcast.half_ref, s32[1]{0:T(128)} %bitcast.3.mine_ref, s32[64,1024]{1,0:T(8,128)} %bitcast.16, bf16[64,16,256]{2,1,0:T(8,128)(2,1)} %bitcast.14, bf16[1024,1024]{1,0:T(8,128)(2,1)} %corpus_hbm.7), custom_call_target="tpu_custom_call" | custom-call | tf_op jit(solution)/shard_map/cross_half/pallas_call | solution.py:64
  13.4 0.6 add.45
  14.0 28.9 %all_to_all.10.pieces_ref = f32[8,64,1024]{2,1,0:T(8,128)S(1)} all-to-all(f32[8,64,1024]{2,1,0:T(8,128)S(1)} %bitcast.12), channel_id=1, replica_groups={{0,1,16,17,64,65,80,81},{3,2,19,18,67,66,83,82},{4,5,20,21,68,69,84,85}..., dimensions={0} | all-to-all | bytes 4194304 | tf_op jit(solution)/shard_map/all_to_all | solution.py:373
  42.9 0.1 pick.1
  43.2 2.5 %collective-permute-start.3 = (f32[16,1024]{1,0:T(8,128)S(1)}, f32[16,1024]{1,0:T(8,128)S(1)}, u32[]{:S(2)}, u32[]{:S(2)}) collective-permute-start(f32[16,1024]{1,0:T(8,128)S(1)} %get-tuple-element.25), channel_id=1, source_target_pairs={{0,48},{1,49},{2,50},{3,51},{4,52},{5,53},{6,54},{7,55},{8,24},{9,... | collective-permute-start | bytes 196616 | tf_op jit(solution)/shard_map/ppermute | solution.py:340
  45.7 1.4 %collective-permute-done.1 = f32[16,1024]{1,0:T(8,128)S(1)} collective-permute-done((f32[16,1024]{1,0:T(8,128)S(1)}, f32[16,1024]{1,0:T(8,128)S(1)}, u32[]{:S(2)}, u32[]{:S(2)}) %collective-permute-start.1) | collective-permute-done | bytes 65568 | tf_op jit(solution)/shard_map/ppermute | solution.py:340
  47.1 0.3 collective-permute-done.3
  47.4 1.7 %collective-permute-start.4 = (f32[16,1024]{1,0:T(8,128)S(1)}, f32[16,1024]{1,0:T(8,128)S(1)}, u32[]{:S(2)}, u32[]{:S(2)}) collective-permute-start(f32[16,1024]{1,0:T(8,128)S(1)} %add_add_fusion.1), channel_id=1, source_target_pairs={{0,4},{1,5},{2,6},{3,7},{4,0},{5,1},{6,2},{7,3},{8,12},{9,13},{10,... | collective-permute-start | bytes 196616 | tf_op jit(solution)/shard_map/ppermute | solution.py:340
  49.1 4.0 %collective-permute-start.6 = (f32[16,1024]{1,0:T(8,128)S(1)}, f32[16,1024]{1,0:T(8,128)S(1)}, u32[]{:S(2)}, u32[]{:S(2)}) collective-permute-start(f32[16,1024]{1,0:T(8,128)S(1)} %add_add_fusion.1), channel_id=1, source_target_pairs={{0,7},{1,2},{2,1},{3,4},{4,3},{5,6},{6,5},{7,0},{8,9},{9,8},{10,11... | collective-permute-start | bytes 196616 | tf_op jit(solution)/shard_map/ppermute | solution.py:340
  53.1 3.2 %distortion.2.sums_ref = f32[1,1024]{1,0:T(1,128)S(1)} custom-call(s32[1]{0:T(128)} %bitcast.6.half_ref, f32[1,1024]{1,0:T(1,128)S(1)} %broadcast_in_dim.3.sums_ref, bf16[1024,1024]{1,0:T(8,128)(2,1)} %rot_hbm.3, bf16[1024,1024]{1,0:T(8,128)(2,1)} %corpus_hbm.7, bf16[512,1024]{1,0:T(8,128)(2,1)S(1)} %copy-done.1), custom_call_target="tpu_custom_call" | custom-call | tf_op jit(solution)/shard_map/distortion/pallas_call | solution.py:144
  56.3 1.3 %collective-permute-done.5 = f32[16,1024]{1,0:T(8,128)S(1)} collective-permute-done((f32[16,1024]{1,0:T(8,128)S(1)}, f32[16,1024]{1,0:T(8,128)S(1)}, u32[]{:S(2)}, u32[]{:S(2)}) %collective-permute-start.5) | collective-permute-done | bytes 65568 | tf_op jit(solution)/shard_map/ppermute | solution.py:340
  57.7 0.6 collective-permute-start.7
  58.2 0.1 collective-permute-start.8
  58.3 2.1 %collective-permute-start.9 = (f32[16,1024]{1,0:T(8,128)S(1)}, f32[16,1024]{1,0:T(8,128)S(1)}, u32[]{:S(2)}, u32[]{:S(2)}) collective-permute-start(f32[16,1024]{1,0:T(8,128)S(1)} %add_add_fusion.refs_0_), channel_id=1, source_target_pairs={{0,240},{1,241},{2,242},{3,243},{4,244},{5,245},{6,246},{7,247},{8... | collective-permute-start | bytes 196616 | tf_op jit(solution)/shard_map/ppermute | solution.py:340
  60.4 0.5 collective-permute-done.7.refs_1_
  60.9 0.5 collective-permute-done.8.refs_2_
  61.3 1.0 collective-permute-done.9.refs_3_
  62.3 0.1 spread.1
  62.5 22.1 %all_to_all.11 = f32[8,64,1024]{2,1,0:T(8,128)S(1)} all-to-all(f32[8,64,1024]{2,1,0:T(8,128)S(1)} %spread.1), channel_id=1, replica_groups={{0,1,16,17,64,65,80,81},{3,2,19,18,67,66,83,82},{4,5,20,21,68,69,84,85}..., dimensions={0} | all-to-all | bytes 4194304 | tf_op jit(solution)/shard_map/all_to_all | solution.py:384
  84.6 4.2 %collective-permute-start.10 = (f32[512,1024]{1,0:T(8,128)S(1)}, f32[512,1024]{1,0:T(8,128)}, u32[]{:S(2)}, u32[]{:S(2)}) collective-permute-start(f32[512,1024]{1,0:T(8,128)S(1)} %bitcast.10), channel_id=1, source_target_pairs={{0,8},{1,9},{2,10},{3,11},{4,12},{5,13},{6,14},{7,15},{8,0},{9,1},... | collective-permute-start | bytes 6291464 | tf_op jit(solution)/shard_map/ppermute | solution.py:340
  88.8 3.8 %distortion.3 = f32[1,1024]{1,0:T(1,128)} custom-call(s32[1]{0:T(128)} %bitcast.half_ref, f32[1,1024]{1,0:T(1,128)S(1)} %distortion.2.sums_ref, bf16[1024,1024]{1,0:T(8,128)(2,1)} %rot_hbm.3, bf16[1024,1024]{1,0:T(8,128)(2,1)} %corpus_hbm.7, bf16[512,1024]{1,0:T(8,128)(2,1)S(1)} %copy-done), custom_call_target="tpu_custom_call" | custom-call | tf_op jit(solution)/shard_map/distortion/pallas_call | solution.py:144
  92.7 21.8 %polar.1 = f32[32,1024]{1,0:T(8,128)} custom-call(s32[3]{0:T(128)S(1)} %pad_add_fusion.place_ref, f32[512,1024]{1,0:T(8,128)S(1)} %bitcast.11, f32[512,1024]{1,0:T(8,128)} %collective-permute-done.10.oth_hbm), custom_call_target="tpu_custom_call" | custom-call | tf_op jit(solution)/shard_map/polar/pallas_call | solution.py:266
  (16 shorter events, 0.4 us)
Async XLA Ops:
  5.4 8.0 %collective-permute-start = (f32[512,1024]{1,0:T(8,128)S(1)}, f32[512,1024]{1,0:T(8,128)S(1)}, u32[]{:S(2)}, u32[]{:S(2)}) collective-permute-start(f32[512,1024]{1,0:T(8,128)S(1)} %get-tuple-element.21), channel_id=1, source_target_pairs={{0,8},{1,9},{2,10},{3,11},{4,12},{5,13},{6,14},{7,15},{8,0},{9,1},... | collective-permute-start | bytes 6291464 | tf_op jit(solution)/shard_map/ppermute | solution.py:340
  42.9 10.3 %copy-start.1 = (bf16[512,1024]{1,0:T(8,128)(2,1)S(1)}, bf16[512,1024]{1,0:T(8,128)(2,1)}, u32[]{:S(2)}) copy-start(bf16[512,1024]{1,0:T(8,128)(2,1)} %get-tuple-element.28.words_hbm) | copy-start | bytes 3145732
  43.0 4.1 %collective-permute-start.1 = (f32[16,1024]{1,0:T(8,128)S(1)}, f32[16,1024]{1,0:T(8,128)S(1)}, u32[]{:S(2)}, u32[]{:S(2)}) collective-permute-start(f32[16,1024]{1,0:T(8,128)S(1)} %get-tuple-element.23), channel_id=1, source_target_pairs={{0,240},{1,241},{2,242},{3,243},{4,244},{5,245},{6,246},{7,247},{8... | collective-permute-start | bytes 196616 | tf_op jit(solution)/shard_map/ppermute | solution.py:340
  43.1 4.0 %collective-permute-start.2 = (f32[16,1024]{1,0:T(8,128)S(1)}, f32[16,1024]{1,0:T(8,128)S(1)}, u32[]{:S(2)}, u32[]{:S(2)}) collective-permute-start(f32[16,1024]{1,0:T(8,128)S(1)} %get-tuple-element.24), channel_id=1, source_target_pairs={{0,192},{1,193},{2,194},{3,195},{4,196},{5,197},{6,198},{7,199},{8... | collective-permute-start | bytes 196616 | tf_op jit(solution)/shard_map/ppermute | solution.py:340
  43.2 4.2 %collective-permute-start.3 = (f32[16,1024]{1,0:T(8,128)S(1)}, f32[16,1024]{1,0:T(8,128)S(1)}, u32[]{:S(2)}, u32[]{:S(2)}) collective-permute-start(f32[16,1024]{1,0:T(8,128)S(1)} %get-tuple-element.25), channel_id=1, source_target_pairs={{0,48},{1,49},{2,50},{3,51},{4,52},{5,53},{6,54},{7,55},{8,24},{9,... | collective-permute-start | bytes 196616 | tf_op jit(solution)/shard_map/ppermute | solution.py:340
  47.4 9.0 %collective-permute-start.4 = (f32[16,1024]{1,0:T(8,128)S(1)}, f32[16,1024]{1,0:T(8,128)S(1)}, u32[]{:S(2)}, u32[]{:S(2)}) collective-permute-start(f32[16,1024]{1,0:T(8,128)S(1)} %add_add_fusion.1), channel_id=1, source_target_pairs={{0,4},{1,5},{2,6},{3,7},{4,0},{5,1},{6,2},{7,3},{8,12},{9,13},{10,... | collective-permute-start | bytes 196616 | tf_op jit(solution)/shard_map/ppermute | solution.py:340
  49.1 8.5 %collective-permute-start.5 = (f32[16,1024]{1,0:T(8,128)S(1)}, f32[16,1024]{1,0:T(8,128)S(1)}, u32[]{:S(2)}, u32[]{:S(2)}) collective-permute-start(f32[16,1024]{1,0:T(8,128)S(1)} %add_add_fusion.1), channel_id=1, source_target_pairs={{0,3},{1,6},{2,5},{3,0},{4,7},{5,2},{6,1},{7,4},{8,13},{9,12},{10,... | collective-permute-start | bytes 196616 | tf_op jit(solution)/shard_map/ppermute | solution.py:340
  49.1 8.5 %collective-permute-start.6 = (f32[16,1024]{1,0:T(8,128)S(1)}, f32[16,1024]{1,0:T(8,128)S(1)}, u32[]{:S(2)}, u32[]{:S(2)}) collective-permute-start(f32[16,1024]{1,0:T(8,128)S(1)} %add_add_fusion.1), channel_id=1, source_target_pairs={{0,7},{1,2},{2,1},{3,4},{4,3},{5,6},{6,5},{7,0},{8,9},{9,8},{10,11... | collective-permute-start | bytes 196616 | tf_op jit(solution)/shard_map/ppermute | solution.py:340
  57.7 3.2 %collective-permute-start.7 = (f32[16,1024]{1,0:T(8,128)S(1)}, f32[16,1024]{1,0:T(8,128)S(1)}, u32[]{:S(2)}, u32[]{:S(2)}) collective-permute-start(f32[16,1024]{1,0:T(8,128)S(1)} %add_add_fusion.refs_0_), channel_id=1, source_target_pairs={{0,48},{1,49},{2,50},{3,51},{4,52},{5,53},{6,54},{7,55},{8,24},{9,... | collective-permute-start | bytes 196616 | tf_op jit(solution)/shard_map/ppermute | solution.py:340
  58.2 3.1 %collective-permute-start.8 = (f32[16,1024]{1,0:T(8,128)S(1)}, f32[16,1024]{1,0:T(8,128)S(1)}, u32[]{:S(2)}, u32[]{:S(2)}) collective-permute-start(f32[16,1024]{1,0:T(8,128)S(1)} %add_add_fusion.refs_0_), channel_id=1, source_target_pairs={{0,192},{1,193},{2,194},{3,195},{4,196},{5,197},{6,198},{7,199},{8... | collective-permute-start | bytes 196616 | tf_op jit(solution)/shard_map/ppermute | solution.py:340
  58.3 4.0 %collective-permute-start.9 = (f32[16,1024]{1,0:T(8,128)S(1)}, f32[16,1024]{1,0:T(8,128)S(1)}, u32[]{:S(2)}, u32[]{:S(2)}) collective-permute-start(f32[16,1024]{1,0:T(8,128)S(1)} %add_add_fusion.refs_0_), channel_id=1, source_target_pairs={{0,240},{1,241},{2,242},{3,243},{4,244},{5,245},{6,246},{7,247},{8... | collective-permute-start | bytes 196616 | tf_op jit(solution)/shard_map/ppermute | solution.py:340
  62.5 26.4 %copy-start = (bf16[512,1024]{1,0:T(8,128)(2,1)S(1)}, bf16[512,1024]{1,0:T(8,128)(2,1)}, u32[]{:S(2)}) copy-start(bf16[512,1024]{1,0:T(8,128)(2,1)} %get-tuple-element.35.words_hbm) | copy-start | bytes 3145732
  84.6 8.1 %collective-permute-start.10 = (f32[512,1024]{1,0:T(8,128)S(1)}, f32[512,1024]{1,0:T(8,128)}, u32[]{:S(2)}, u32[]{:S(2)}) collective-permute-start(f32[512,1024]{1,0:T(8,128)S(1)} %bitcast.10), channel_id=1, source_target_pairs={{0,8},{1,9},{2,10},{3,11},{4,12},{5,13},{6,14},{7,15},{8,0},{9,1},... | collective-permute-start | bytes 6291464 | tf_op jit(solution)/shard_map/ppermute | solution.py:340

commit v4 on v3

--- a/solution.py
+++ b/solution.py
@@ -76,6 +76,35 @@
         compiler_params=pltpu.CompilerParams(vmem_limit_bytes=24 * MIB),
         name="cross_half",
     )(half, mine, codes_t, books_t, corpus)
+
+
+def second_kernel(scale, half_ref, codes_ref, books_ref, corpus_ref, out_ref, words_hbm, words, sem):
+    subs = books_ref.shape[0] // 2
+    first = pl.multiple_of(half_ref[0] * subs, subs)
+    at = pl.ds(first, subs)
+    for block in range(subs // CHUNK):
+        rebuild(codes_ref.at[at], books_ref.at[at], words, block)
+    store = pltpu.make_async_copy(words, words_hbm, sem)
+    store.start()
+    for k in range(corpus_ref.shape[1] // BLK):
+        c = slice(k * BLK, (k + 1) * BLK)
+        out_ref[:, c] = nn(words[...], corpus_ref[:, c]) * scale
+    store.wait()
+
+
+def cross_second(half, codes_t, books_t, corpus, scale):
+    subs, width, _ = books_t.shape
+    rows, d = corpus.shape
+    part = subs // 2
+    return pl.pallas_call(
+        functools.partial(second_kernel, scale),
+        in_specs=[pl.BlockSpec(memory_space=pltpu.SMEM)] + [pl.BlockSpec(memory_space=pltpu.VMEM)] * 3,
+        out_specs=[pl.BlockSpec(memory_space=pltpu.VMEM), pl.BlockSpec(memory_space=pltpu.HBM)],
+        out_shape=[jax.ShapeDtypeStruct((part * width, d), F32), pltpu.HBM((part * width, rows), BF)],
+        scratch_shapes=[pltpu.VMEM((part * width, rows), BF), pltpu.SemaphoreType.DMA],
+        compiler_params=pltpu.CompilerParams(vmem_limit_bytes=16 * MIB),
+        name="cross_second",
+    )(half, codes_t, books_t, corpus)
 
 
 def pick_kernel(mine_ref, pieces_ref, *out_refs):
@@ -365,7 +394,7 @@
     far_half, near_half = (1 - core).reshape(1), core.reshape(1)
     far_term, far_words = cross_half(far_half, mine, held[0], held[1], held[2], scale)
     arrived = send(far_term, SWAP_CORE)
-    near_term, near_words = cross_half(near_half, mine, held[0], held[1], held[2], scale)
+    near_term, near_words = cross_second(near_half, codes_t, books_t, corpus, scale)
 
     groups = cube_groups()
     members = len(groups[0])

time: 115 us -> 115 us (level)
    pallas_call x2 -> x1, Pallas kernels: 9.36 us -> 4.82 us  [cross_half(): pl.pallas_call(functools.partial(first_kernel, scale), in_specs=[pl.Block...]
    pallas_call x0 -> x1, Pallas kernels: none -> 3.45 us  [cross_second(): pl.pallas_call(functools.partial(second_kernel, scale), in_specs=[pl.Bloc...]
  transfers between devices with their start and end apart: 11 -> 11, of which waited for: 6 -> 7; matrix products, arithmetic and copies ran while one was open for 0% -> 0% of each run, Pallas kernels for 10% -> 9%
where the time goes in v4:
time: 115 us; the launch traced here: 114 us
  blocking collectives  50.7 us (44%)
  Pallas kernels  37.3 us (32%)
  starting transfers between devices  19 us (17%)
  waiting for transfers between devices  5.78 us (5%)
    all_to_all x1, blocking collectives, body(): pieces = lax.all_to_all(summed, AXES, 0, 0, axis_index_groups=groups)  28.9 us
    all_to_all x1, blocking collectives, body(): own = lax.all_to_all(gathered, AXES, 0, 0, axis_index_groups=groups)  21.9 us
    pallas_call x1, Pallas kernels, polar(): pl.pallas_call(functools.partial(polar_kernel, polar_polynomial(ITERS)),...  21.8 us
    ppermute x11, starting transfers between devices, send(): return lax.ppermute(value, AXES, pairs)  19 us
    pallas_call x2, Pallas kernels, distortion(): pl.pallas_call(dist_kernel, in_specs=[pl.BlockSpec(memory_space=pltpu.SME...  6.97 us
    ppermute x11, waiting for transfers between devices, send(): return lax.ppermute(value, AXES, pairs)  5.78 us
    pallas_call x1, Pallas kernels, cross_half(): pl.pallas_call(functools.partial(first_kernel, scale), in_specs=[pl.Block...  4.82 us
    pallas_call x1, Pallas kernels, cross_second(): pl.pallas_call(functools.partial(second_kernel, scale), in_specs=[pl.Bloc...  3.45 us
  transfers between devices with their start and end apart: 11, of which 7 were waited for; matrix products, arithmetic and copies ran while one was open for 0% of the time, Pallas kernels for 9%

profile of v4, /device:TPU:1, one launch (start us, length us, event | category | flops | bytes accessed | tf_op | source)
XLA Modules:
  0.0 114.5 jit_solution(616595117794718430)
XLA Ops:
  0.7 4.8 %cross_half.1 = (f32[512,1024]{1,0:T(8,128)S(1)}, bf16[512,1024]{1,0:T(8,128)(2,1)}) custom-call(s32[1]{0:T(128)} %bitcast.6.half_ref, s32[1]{0:T(128)} %bitcast.3.mine_ref, s32[64,1024]{1,0:T(8,128)} %bitcast.14, bf16[64,16,256]{2,1,0:T(8,128)(2,1)} %bitcast.12, bf16[1024,1024]{1,0:T(8,128)(2,1)} %corpus_hbm.5), custom_call_target="tpu_custom_call" | custom-call | tf_op jit(solution)/shard_map/cross_half/pallas_call | solution.py:64
  5.6 3.3 %collective-permute-start = (f32[512,1024]{1,0:T(8,128)S(1)}, f32[512,1024]{1,0:T(8,128)S(1)}, u32[]{:S(2)}, u32[]{:S(2)}) collective-permute-start(f32[512,1024]{1,0:T(8,128)S(1)} %get-tuple-element.21), channel_id=1, source_target_pairs={{0,8},{1,9},{2,10},{3,11},{4,12},{5,13},{6,14},{7,15},{8,0},{9,1},... | collective-permute-start | bytes 6291464 | tf_op jit(solution)/shard_map/ppermute | solution.py:369
  8.9 3.5 %cross_second.1 = (f32[512,1024]{1,0:T(8,128)S(1)}, bf16[512,1024]{1,0:T(8,128)(2,1)}) custom-call(s32[1]{0:T(128)} %bitcast.half_ref, s32[64,1024]{1,0:T(8,128)S(1)} %bitcast.15, bf16[64,16,256]{2,1,0:T(8,128)(2,1)S(1)} %bitcast.13, bf16[1024,1024]{1,0:T(8,128)(2,1)S(1)} %copy-done), custom_call_target="tpu_custom_call" | custom-call | tf_op jit(solution)/shard_map/cross_second/pallas_call | solution.py:99
  12.4 0.3 collective-permute-done
  12.7 0.5 add.45
  13.2 28.9 %all_to_all.10.pieces_ref = f32[8,64,1024]{2,1,0:T(8,128)S(1)} all-to-all(f32[8,64,1024]{2,1,0:T(8,128)S(1)} %bitcast.16), channel_id=1, replica_groups={{0,1,16,17,64,65,80,81},{3,2,19,18,67,66,83,82},{4,5,20,21,68,69,84,85}..., dimensions={0} | all-to-all | bytes 4194304 | tf_op jit(solution)/shard_map/all_to_all | solution.py:402
  42.4 2.5 %collective-permute-start.3 = (f32[16,1024]{1,0:T(8,128)S(1)}, f32[16,1024]{1,0:T(8,128)S(1)}, u32[]{:S(2)}, u32[]{:S(2)}) collective-permute-start(f32[16,1024]{1,0:T(8,128)S(1)} %get-tuple-element.25), channel_id=1, source_target_pairs={{0,48},{1,49},{2,50},{3,51},{4,52},{5,53},{6,54},{7,55},{8,24},{9,... | collective-permute-start | bytes 196616 | tf_op jit(solution)/shard_map/ppermute | solution.py:369
  45.0 1.4 %collective-permute-done.1 = f32[16,1024]{1,0:T(8,128)S(1)} collective-permute-done((f32[16,1024]{1,0:T(8,128)S(1)}, f32[16,1024]{1,0:T(8,128)S(1)}, u32[]{:S(2)}, u32[]{:S(2)}) %collective-permute-start.1) | collective-permute-done | bytes 65568 | tf_op jit(solution)/shard_map/ppermute | solution.py:369
  46.3 0.3 collective-permute-done.3
  46.6 2.0 %collective-permute-start.4 = (f32[16,1024]{1,0:T(8,128)S(1)}, f32[16,1024]{1,0:T(8,128)S(1)}, u32[]{:S(2)}, u32[]{:S(2)}) collective-permute-start(f32[16,1024]{1,0:T(8,128)S(1)} %add_add_fusion.1), channel_id=1, source_target_pairs={{0,4},{1,5},{2,6},{3,7},{4,0},{5,1},{6,2},{7,3},{8,12},{9,13},{10,... | collective-permute-start | bytes 196616 | tf_op jit(solution)/shard_map/ppermute | solution.py:369
  48.6 3.8 %collective-permute-start.6 = (f32[16,1024]{1,0:T(8,128)S(1)}, f32[16,1024]{1,0:T(8,128)S(1)}, u32[]{:S(2)}, u32[]{:S(2)}) collective-permute-start(f32[16,1024]{1,0:T(8,128)S(1)} %add_add_fusion.1), channel_id=1, source_target_pairs={{0,7},{1,2},{2,1},{3,4},{4,3},{5,6},{6,5},{7,0},{8,9},{9,8},{10,11... | collective-permute-start | bytes 196616 | tf_op jit(solution)/shard_map/ppermute | solution.py:369
  52.4 3.2 %distortion.2.sums_ref = f32[1,1024]{1,0:T(1,128)S(1)} custom-call(s32[1]{0:T(128)} %bitcast.6.half_ref, f32[1,1024]{1,0:T(1,128)S(1)} %broadcast_in_dim.3.sums_ref, bf16[1024,1024]{1,0:T(8,128)(2,1)} %rot_hbm.3, bf16[1024,1024]{1,0:T(8,128)(2,1)} %corpus_hbm.5, bf16[512,1024]{1,0:T(8,128)(2,1)S(1)} %copy-done.3), custom_call_target="tpu_custom_call" | custom-call | tf_op jit(solution)/shard_map/distortion/pallas_call | solution.py:173
  55.6 0.8 collective-permute-done.5
  56.4 1.2 %collective-permute-start.7 = (f32[16,1024]{1,0:T(8,128)S(1)}, f32[16,1024]{1,0:T(8,128)S(1)}, u32[]{:S(2)}, u32[]{:S(2)}) collective-permute-start(f32[16,1024]{1,0:T(8,128)S(1)} %add_add_fusion.refs_0_), channel_id=1, source_target_pairs={{0,48},{1,49},{2,50},{3,51},{4,52},{5,53},{6,54},{7,55},{8,24},{9,... | collective-permute-start | bytes 196616 | tf_op jit(solution)/shard_map/ppermute | solution.py:369
  57.6 0.6 collective-permute-start.8
  58.3 1.1 collective-permute-start.9
  59.4 0.4 collective-permute-done.7.refs_1_
  59.8 0.9 collective-permute-done.8.refs_2_
  60.8 1.5 %collective-permute-done.9.refs_3_ = f32[16,1024]{1,0:T(8,128)S(1)} collective-permute-done((f32[16,1024]{1,0:T(8,128)S(1)}, f32[16,1024]{1,0:T(8,128)S(1)}, u32[]{:S(2)}, u32[]{:S(2)}) %collective-permute-start.9) | collective-permute-done | bytes 65568 | tf_op jit(solution)/shard_map/ppermute | solution.py:369
  62.3 0.1 spread.1
  62.5 21.9 %all_to_all.11 = f32[8,64,1024]{2,1,0:T(8,128)S(1)} all-to-all(f32[8,64,1024]{2,1,0:T(8,128)S(1)} %spread.1), channel_id=1, replica_groups={{0,1,16,17,64,65,80,81},{3,2,19,18,67,66,83,82},{4,5,20,21,68,69,84,85}..., dimensions={0} | all-to-all | bytes 4194304 | tf_op jit(solution)/shard_map/all_to_all | solution.py:413
  84.3 4.2 %collective-permute-start.10 = (f32[512,1024]{1,0:T(8,128)S(1)}, f32[512,1024]{1,0:T(8,128)}, u32[]{:S(2)}, u32[]{:S(2)}) collective-permute-start(f32[512,1024]{1,0:T(8,128)S(1)} %bitcast.10), channel_id=1, source_target_pairs={{0,8},{1,9},{2,10},{3,11},{4,12},{5,13},{6,14},{7,15},{8,0},{9,1},... | collective-permute-start | bytes 6291464 | tf_op jit(solution)/shard_map/ppermute | solution.py:369
  88.6 3.8 %distortion.3 = f32[1,1024]{1,0:T(1,128)} custom-call(s32[1]{0:T(128)} %bitcast.half_ref, f32[1,1024]{1,0:T(1,128)S(1)} %distortion.2.sums_ref, bf16[1024,1024]{1,0:T(8,128)(2,1)} %rot_hbm.3, bf16[1024,1024]{1,0:T(8,128)(2,1)} %corpus_hbm.5, bf16[512,1024]{1,0:T(8,128)(2,1)S(1)} %copy-done.2), custom_call_target="tpu_custom_call" | custom-call | tf_op jit(solution)/shard_map/distortion/pallas_call | solution.py:173
  92.5 21.8 %polar.1 = f32[32,1024]{1,0:T(8,128)} custom-call(s32[3]{0:T(128)S(1)} %pad_add_fusion.place_ref, f32[512,1024]{1,0:T(8,128)S(1)} %bitcast.11, f32[512,1024]{1,0:T(8,128)} %collective-permute-done.10.oth_hbm), custom_call_target="tpu_custom_call" | custom-call | tf_op jit(solution)/shard_map/polar/pallas_call | solution.py:295
  (22 shorter events, 0.5 us)
Async XLA Ops:
  0.6 8.3 %copy-start.4 = (s32[1024,64]{0,1:T(8,128)S(1)}, s32[1024,64]{0,1:T(8,128)}, u32[]{:S(2)}) copy-start(s32[1024,64]{0,1:T(8,128)} %param.6) | copy-start | bytes 786436
  0.6 8.3 %copy-start.1 = (bf16[64,256,16]{1,2,0:T(8,128)(2,1)S(1)}, bf16[64,256,16]{1,2,0:T(8,128)(2,1)}, u32[]{:S(2)}) copy-start(bf16[64,256,16]{1,2,0:T(8,128)(2,1)} %param.7) | copy-start | bytes 1572868
  0.6 8.2 %copy-start = (bf16[1024,1024]{1,0:T(8,128)(2,1)S(1)}, bf16[1024,1024]{1,0:T(8,128)(2,1)}, u32[]{:S(2)}) copy-start(bf16[1024,1024]{1,0:T(8,128)(2,1)} %corpus_hbm.5) | copy-start | bytes 6291460
  5.6 7.1 %collective-permute-start = (f32[512,1024]{1,0:T(8,128)S(1)}, f32[512,1024]{1,0:T(8,128)S(1)}, u32[]{:S(2)}, u32[]{:S(2)}) collective-permute-start(f32[512,1024]{1,0:T(8,128)S(1)} %get-tuple-element.21), channel_id=1, source_target_pairs={{0,8},{1,9},{2,10},{3,11},{4,12},{5,13},{6,14},{7,15},{8,0},{9,1},... | collective-permute-start | bytes 6291464 | tf_op jit(solution)/shard_map/ppermute | solution.py:369
  42.1 10.3 %copy-start.3 = (bf16[512,1024]{1,0:T(8,128)(2,1)S(1)}, bf16[512,1024]{1,0:T(8,128)(2,1)}, u32[]{:S(2)}) copy-start(bf16[512,1024]{1,0:T(8,128)(2,1)} %get-tuple-element.28.words_hbm) | copy-start | bytes 3145732
  42.2 4.1 %collective-permute-start.1 = (f32[16,1024]{1,0:T(8,128)S(1)}, f32[16,1024]{1,0:T(8,128)S(1)}, u32[]{:S(2)}, u32[]{:S(2)}) collective-permute-start(f32[16,1024]{1,0:T(8,128)S(1)} %get-tuple-element.23), channel_id=1, source_target_pairs={{0,240},{1,241},{2,242},{3,243},{4,244},{5,245},{6,246},{7,247},{8... | collective-permute-start | bytes 196616 | tf_op jit(solution)/shard_map/ppermute | solution.py:369
  42.3 4.0 %collective-permute-start.2 = (f32[16,1024]{1,0:T(8,128)S(1)}, f32[16,1024]{1,0:T(8,128)S(1)}, u32[]{:S(2)}, u32[]{:S(2)}) collective-permute-start(f32[16,1024]{1,0:T(8,128)S(1)} %get-tuple-element.24), channel_id=1, source_target_pairs={{0,192},{1,193},{2,194},{3,195},{4,196},{5,197},{6,198},{7,199},{8... | collective-permute-start | bytes 196616 | tf_op jit(solution)/shard_map/ppermute | solution.py:369
  42.4 4.2 %collective-permute-start.3 = (f32[16,1024]{1,0:T(8,128)S(1)}, f32[16,1024]{1,0:T(8,128)S(1)}, u32[]{:S(2)}, u32[]{:S(2)}) collective-permute-start(f32[16,1024]{1,0:T(8,128)S(1)} %get-tuple-element.25), channel_id=1, source_target_pairs={{0,48},{1,49},{2,50},{3,51},{4,52},{5,53},{6,54},{7,55},{8,24},{9,... | collective-permute-start | bytes 196616 | tf_op jit(solution)/shard_map/ppermute | solution.py:369
  46.6 9.0 %collective-permute-start.4 = (f32[16,1024]{1,0:T(8,128)S(1)}, f32[16,1024]{1,0:T(8,128)S(1)}, u32[]{:S(2)}, u32[]{:S(2)}) collective-permute-start(f32[16,1024]{1,0:T(8,128)S(1)} %add_add_fusion.1), channel_id=1, source_target_pairs={{0,4},{1,5},{2,6},{3,7},{4,0},{5,1},{6,2},{7,3},{8,12},{9,13},{10,... | collective-permute-start | bytes 196616 | tf_op jit(solution)/shard_map/ppermute | solution.py:369
  48.6 7.8 %collective-permute-start.5 = (f32[16,1024]{1,0:T(8,128)S(1)}, f32[16,1024]{1,0:T(8,128)S(1)}, u32[]{:S(2)}, u32[]{:S(2)}) collective-permute-start(f32[16,1024]{1,0:T(8,128)S(1)} %add_add_fusion.1), channel_id=1, source_target_pairs={{0,3},{1,6},{2,5},{3,0},{4,7},{5,2},{6,1},{7,4},{8,13},{9,12},{10,... | collective-permute-start | bytes 196616 | tf_op jit(solution)/shard_map/ppermute | solution.py:369
  48.6 7.8 %collective-permute-start.6 = (f32[16,1024]{1,0:T(8,128)S(1)}, f32[16,1024]{1,0:T(8,128)S(1)}, u32[]{:S(2)}, u32[]{:S(2)}) collective-permute-start(f32[16,1024]{1,0:T(8,128)S(1)} %add_add_fusion.1), channel_id=1, source_target_pairs={{0,7},{1,2},{2,1},{3,4},{4,3},{5,6},{6,5},{7,0},{8,9},{9,8},{10,11... | collective-permute-start | bytes 196616 | tf_op jit(solution)/shard_map/ppermute | solution.py:369
  56.4 3.4 %collective-permute-start.7 = (f32[16,1024]{1,0:T(8,128)S(1)}, f32[16,1024]{1,0:T(8,128)S(1)}, u32[]{:S(2)}, u32[]{:S(2)}) collective-permute-start(f32[16,1024]{1,0:T(8,128)S(1)} %add_add_fusion.refs_0_), channel_id=1, source_target_pairs={{0,48},{1,49},{2,50},{3,51},{4,52},{5,53},{6,54},{7,55},{8,24},{9,... | collective-permute-start | bytes 196616 | tf_op jit(solution)/shard_map/ppermute | solution.py:369
  57.6 3.1 %collective-permute-start.8 = (f32[16,1024]{1,0:T(8,128)S(1)}, f32[16,1024]{1,0:T(8,128)S(1)}, u32[]{:S(2)}, u32[]{:S(2)}) collective-permute-start(f32[16,1024]{1,0:T(8,128)S(1)} %add_add_fusion.refs_0_), channel_id=1, source_target_pairs={{0,192},{1,193},{2,194},{3,195},{4,196},{5,197},{6,198},{7,199},{8... | collective-permute-start | bytes 196616 | tf_op jit(solution)/shard_map/ppermute | solution.py:369
  58.3 4.0 %collective-permute-start.9 = (f32[16,1024]{1,0:T(8,128)S(1)}, f32[16,1024]{1,0:T(8,128)S(1)}, u32[]{:S(2)}, u32[]{:S(2)}) collective-permute-start(f32[16,1024]{1,0:T(8,128)S(1)} %add_add_fusion.refs_0_), channel_id=1, source_target_pairs={{0,240},{1,241},{2,242},{3,243},{4,244},{5,245},{6,246},{7,247},{8... | collective-permute-start | bytes 196616 | tf_op jit(solution)/shard_map/ppermute | solution.py:369
  62.5 26.2 %copy-start.2 = (bf16[512,1024]{1,0:T(8,128)(2,1)S(1)}, bf16[512,1024]{1,0:T(8,128)(2,1)}, u32[]{:S(2)}) copy-start(bf16[512,1024]{1,0:T(8,128)(2,1)} %get-tuple-element.35.words_hbm) | copy-start | bytes 3145732
  84.3 8.2 %collective-permute-start.10 = (f32[512,1024]{1,0:T(8,128)S(1)}, f32[512,1024]{1,0:T(8,128)}, u32[]{:S(2)}, u32[]{:S(2)}) collective-permute-start(f32[512,1024]{1,0:T(8,128)S(1)} %bitcast.10), channel_id=1, source_target_pairs={{0,8},{1,9},{2,10},{3,11},{4,12},{5,13},{6,14},{7,15},{8,0},{9,1},... | collective-permute-start | bytes 6291464 | tf_op jit(solution)/shard_map/ppermute | solution.py:369

commit v5 on v4

--- a/solution.py
+++ b/solution.py
@@ -9,6 +9,7 @@
 BF, F32 = jnp.bfloat16, jnp.float32
 MIB = 1 << 20
 BLK = 256
+COARSE = 5
 ITERS = 4
 CHUNK = 16
 
@@ -282,7 +283,8 @@
 
     u = mix((len(coef) - 1) // 4)
     for k in range((len(coef) - 1) // 4 - 1, -1, -1):
-        u = u - thin(u, yh, yl) + mix(k)
+        step = nn(u.astype(BF), yh[...]) if k >= COARSE else thin(u, yh, yl)
+        u = u - step + mix(k)
     u = u * math.sqrt(n)
     low = place_ref[0] == 0
     out_ref[:, :half] = jnp.where(low, u[:, :half], u[:, half:])

time: 115 us -> 113 us (0.983)
  Pallas kernels: 37.3 us -> 35.5 us
    pallas_call x1, Pallas kernels: 21.8 us -> 20 us  [polar(): pl.pallas_call(functools.partial(polar_kernel, polar_polynomial(ITERS)),...]
where the time goes in v5:
time: 113 us
  blocking collectives  50.7 us (45%)
  Pallas kernels  35.5 us (31%)
  starting transfers between devices  19 us (17%)
  waiting for transfers between devices  5.78 us (5%)
    all_to_all x1, blocking collectives, body(): pieces = lax.all_to_all(summed, AXES, 0, 0, axis_index_groups=groups)  28.9 us
    all_to_all x1, blocking collectives, body(): own = lax.all_to_all(gathered, AXES, 0, 0, axis_index_groups=groups)  21.9 us
    pallas_call x1, Pallas kernels, polar(): pl.pallas_call(functools.partial(polar_kernel, polar_polynomial(ITERS)),...  20 us
    ppermute x11, starting transfers between devices, send(): return lax.ppermute(value, AXES, pairs)  19 us
    pallas_call x2, Pallas kernels, distortion(): pl.pallas_call(dist_kernel, in_specs=[pl.BlockSpec(memory_space=pltpu.SME...  6.97 us
    ppermute x11, waiting for transfers between devices, send(): return lax.ppermute(value, AXES, pairs)  5.78 us
    pallas_call x1, Pallas kernels, cross_half(): pl.pallas_call(functools.partial(first_kernel, scale), in_specs=[pl.Block...  4.82 us
    pallas_call x1, Pallas kernels, cross_second(): pl.pallas_call(functools.partial(second_kernel, scale), in_specs=[pl.Bloc...  3.45 us
  transfers between devices with their start and end apart: 11, of which 7 were waited for; matrix products, arithmetic and copies ran while one was open for 0% of the time, Pallas kernels for 9%

profile of v5, /device:TPU:1, one launch (start us, length us, event | category | flops | bytes accessed | tf_op | source)
XLA Modules:
  0.0 112.7 jit_solution(1042672505548223930)
XLA Ops:
  0.7 4.8 %cross_half.1 = (f32[512,1024]{1,0:T(8,128)S(1)}, bf16[512,1024]{1,0:T(8,128)(2,1)}) custom-call(s32[1]{0:T(128)} %bitcast.6.half_ref, s32[1]{0:T(128)} %bitcast.3.mine_ref, s32[64,1024]{1,0:T(8,128)} %bitcast.14, bf16[64,16,256]{2,1,0:T(8,128)(2,1)} %bitcast.12, bf16[1024,1024]{1,0:T(8,128)(2,1)} %corpus_hbm.5), custom_call_target="tpu_custom_call" | custom-call | tf_op jit(solution)/shard_map/cross_half/pallas_call | solution.py:65
  5.6 3.3 %collective-permute-start = (f32[512,1024]{1,0:T(8,128)S(1)}, f32[512,1024]{1,0:T(8,128)S(1)}, u32[]{:S(2)}, u32[]{:S(2)}) collective-permute-start(f32[512,1024]{1,0:T(8,128)S(1)} %get-tuple-element.21), channel_id=1, source_target_pairs={{0,8},{1,9},{2,10},{3,11},{4,12},{5,13},{6,14},{7,15},{8,0},{9,1},... | collective-permute-start | bytes 6291464 | tf_op jit(solution)/shard_map/ppermute | solution.py:371
  8.9 3.5 %cross_second.1 = (f32[512,1024]{1,0:T(8,128)S(1)}, bf16[512,1024]{1,0:T(8,128)(2,1)}) custom-call(s32[1]{0:T(128)} %bitcast.half_ref, s32[64,1024]{1,0:T(8,128)S(1)} %bitcast.15, bf16[64,16,256]{2,1,0:T(8,128)(2,1)S(1)} %bitcast.13, bf16[1024,1024]{1,0:T(8,128)(2,1)S(1)} %copy-done), custom_call_target="tpu_custom_call" | custom-call | tf_op jit(solution)/shard_map/cross_second/pallas_call | solution.py:100
  12.4 0.3 collective-permute-done
  12.7 0.5 add.45
  13.2 28.9 %all_to_all.10.pieces_ref = f32[8,64,1024]{2,1,0:T(8,128)S(1)} all-to-all(f32[8,64,1024]{2,1,0:T(8,128)S(1)} %bitcast.16), channel_id=1, replica_groups={{0,1,16,17,64,65,80,81},{3,2,19,18,67,66,83,82},{4,5,20,21,68,69,84,85}..., dimensions={0} | all-to-all | bytes 4194304 | tf_op jit(solution)/shard_map/all_to_all | solution.py:404
  42.4 2.5 %collective-permute-start.3 = (f32[16,1024]{1,0:T(8,128)S(1)}, f32[16,1024]{1,0:T(8,128)S(1)}, u32[]{:S(2)}, u32[]{:S(2)}) collective-permute-start(f32[16,1024]{1,0:T(8,128)S(1)} %get-tuple-element.25), channel_id=1, source_target_pairs={{0,48},{1,49},{2,50},{3,51},{4,52},{5,53},{6,54},{7,55},{8,24},{9,... | collective-permute-start | bytes 196616 | tf_op jit(solution)/shard_map/ppermute | solution.py:371
  45.0 1.4 %collective-permute-done.1 = f32[16,1024]{1,0:T(8,128)S(1)} collective-permute-done((f32[16,1024]{1,0:T(8,128)S(1)}, f32[16,1024]{1,0:T(8,128)S(1)}, u32[]{:S(2)}, u32[]{:S(2)}) %collective-permute-start.1) | collective-permute-done | bytes 65568 | tf_op jit(solution)/shard_map/ppermute | solution.py:371
  46.3 0.3 collective-permute-done.3
  46.6 2.0 %collective-permute-start.4 = (f32[16,1024]{1,0:T(8,128)S(1)}, f32[16,1024]{1,0:T(8,128)S(1)}, u32[]{:S(2)}, u32[]{:S(2)}) collective-permute-start(f32[16,1024]{1,0:T(8,128)S(1)} %add_add_fusion.1), channel_id=1, source_target_pairs={{0,4},{1,5},{2,6},{3,7},{4,0},{5,1},{6,2},{7,3},{8,12},{9,13},{10,... | collective-permute-start | bytes 196616 | tf_op jit(solution)/shard_map/ppermute | solution.py:371
  48.6 3.8 %collective-permute-start.6 = (f32[16,1024]{1,0:T(8,128)S(1)}, f32[16,1024]{1,0:T(8,128)S(1)}, u32[]{:S(2)}, u32[]{:S(2)}) collective-permute-start(f32[16,1024]{1,0:T(8,128)S(1)} %add_add_fusion.1), channel_id=1, source_target_pairs={{0,7},{1,2},{2,1},{3,4},{4,3},{5,6},{6,5},{7,0},{8,9},{9,8},{10,11... | collective-permute-start | bytes 196616 | tf_op jit(solution)/shard_map/ppermute | solution.py:371
  52.4 3.2 %distortion.2.sums_ref = f32[1,1024]{1,0:T(1,128)S(1)} custom-call(s32[1]{0:T(128)} %bitcast.6.half_ref, f32[1,1024]{1,0:T(1,128)S(1)} %broadcast_in_dim.3.sums_ref, bf16[1024,1024]{1,0:T(8,128)(2,1)} %rot_hbm.3, bf16[1024,1024]{1,0:T(8,128)(2,1)} %corpus_hbm.5, bf16[512,1024]{1,0:T(8,128)(2,1)S(1)} %copy-done.3), custom_call_target="tpu_custom_call" | custom-call | tf_op jit(solution)/shard_map/distortion/pallas_call | solution.py:174
  55.6 0.8 collective-permute-done.5
  56.4 1.2 %collective-permute-start.7 = (f32[16,1024]{1,0:T(8,128)S(1)}, f32[16,1024]{1,0:T(8,128)S(1)}, u32[]{:S(2)}, u32[]{:S(2)}) collective-permute-start(f32[16,1024]{1,0:T(8,128)S(1)} %add_add_fusion.refs_0_), channel_id=1, source_target_pairs={{0,48},{1,49},{2,50},{3,51},{4,52},{5,53},{6,54},{7,55},{8,24},{9,... | collective-permute-start | bytes 196616 | tf_op jit(solution)/shard_map/ppermute | solution.py:371
  57.6 0.6 collective-permute-start.8
  58.3 1.1 collective-permute-start.9
  59.4 0.4 collective-permute-done.7.refs_1_
  59.8 0.9 collective-permute-done.8.refs_2_
  60.8 1.5 %collective-permute-done.9.refs_3_ = f32[16,1024]{1,0:T(8,128)S(1)} collective-permute-done((f32[16,1024]{1,0:T(8,128)S(1)}, f32[16,1024]{1,0:T(8,128)S(1)}, u32[]{:S(2)}, u32[]{:S(2)}) %collective-permute-start.9) | collective-permute-done | bytes 65568 | tf_op jit(solution)/shard_map/ppermute | solution.py:371
  62.3 0.1 spread.1
  62.5 21.9 %all_to_all.11 = f32[8,64,1024]{2,1,0:T(8,128)S(1)} all-to-all(f32[8,64,1024]{2,1,0:T(8,128)S(1)} %spread.1), channel_id=1, replica_groups={{0,1,16,17,64,65,80,81},{3,2,19,18,67,66,83,82},{4,5,20,21,68,69,84,85}..., dimensions={0} | all-to-all | bytes 4194304 | tf_op jit(solution)/shard_map/all_to_all | solution.py:415
  84.3 4.2 %collective-permute-start.10 = (f32[512,1024]{1,0:T(8,128)S(1)}, f32[512,1024]{1,0:T(8,128)}, u32[]{:S(2)}, u32[]{:S(2)}) collective-permute-start(f32[512,1024]{1,0:T(8,128)S(1)} %bitcast.10), channel_id=1, source_target_pairs={{0,8},{1,9},{2,10},{3,11},{4,12},{5,13},{6,14},{7,15},{8,0},{9,1},... | collective-permute-start | bytes 6291464 | tf_op jit(solution)/shard_map/ppermute | solution.py:371
  88.6 3.8 %distortion.3 = f32[1,1024]{1,0:T(1,128)} custom-call(s32[1]{0:T(128)} %bitcast.half_ref, f32[1,1024]{1,0:T(1,128)S(1)} %distortion.2.sums_ref, bf16[1024,1024]{1,0:T(8,128)(2,1)} %rot_hbm.3, bf16[1024,1024]{1,0:T(8,128)(2,1)} %corpus_hbm.5, bf16[512,1024]{1,0:T(8,128)(2,1)S(1)} %copy-done.2), custom_call_target="tpu_custom_call" | custom-call | tf_op jit(solution)/shard_map/distortion/pallas_call | solution.py:174
  92.5 20.0 %polar.1 = f32[32,1024]{1,0:T(8,128)} custom-call(s32[3]{0:T(128)S(1)} %pad_add_fusion.place_ref, f32[512,1024]{1,0:T(8,128)S(1)} %bitcast.11, f32[512,1024]{1,0:T(8,128)} %collective-permute-done.10.oth_hbm), custom_call_target="tpu_custom_call" | custom-call | tf_op jit(solution)/shard_map/polar/pallas_call | solution.py:297
  (22 shorter events, 0.5 us)
Async XLA Ops:
  0.6 8.3 %copy-start.4 = (s32[1024,64]{0,1:T(8,128)S(1)}, s32[1024,64]{0,1:T(8,128)}, u32[]{:S(2)}) copy-start(s32[1024,64]{0,1:T(8,128)} %param.6) | copy-start | bytes 786436
  0.6 8.3 %copy-start.1 = (bf16[64,256,16]{1,2,0:T(8,128)(2,1)S(1)}, bf16[64,256,16]{1,2,0:T(8,128)(2,1)}, u32[]{:S(2)}) copy-start(bf16[64,256,16]{1,2,0:T(8,128)(2,1)} %param.7) | copy-start | bytes 1572868
  0.6 8.2 %copy-start = (bf16[1024,1024]{1,0:T(8,128)(2,1)S(1)}, bf16[1024,1024]{1,0:T(8,128)(2,1)}, u32[]{:S(2)}) copy-start(bf16[1024,1024]{1,0:T(8,128)(2,1)} %corpus_hbm.5) | copy-start | bytes 6291460
  5.6 7.1 %collective-permute-start = (f32[512,1024]{1,0:T(8,128)S(1)}, f32[512,1024]{1,0:T(8,128)S(1)}, u32[]{:S(2)}, u32[]{:S(2)}) collective-permute-start(f32[512,1024]{1,0:T(8,128)S(1)} %get-tuple-element.21), channel_id=1, source_target_pairs={{0,8},{1,9},{2,10},{3,11},{4,12},{5,13},{6,14},{7,15},{8,0},{9,1},... | collective-permute-start | bytes 6291464 | tf_op jit(solution)/shard_map/ppermute | solution.py:371
  42.1 10.3 %copy-start.3 = (bf16[512,1024]{1,0:T(8,128)(2,1)S(1)}, bf16[512,1024]{1,0:T(8,128)(2,1)}, u32[]{:S(2)}) copy-start(bf16[512,1024]{1,0:T(8,128)(2,1)} %get-tuple-element.28.words_hbm) | copy-start | bytes 3145732
  42.2 4.1 %collective-permute-start.1 = (f32[16,1024]{1,0:T(8,128)S(1)}, f32[16,1024]{1,0:T(8,128)S(1)}, u32[]{:S(2)}, u32[]{:S(2)}) collective-permute-start(f32[16,1024]{1,0:T(8,128)S(1)} %get-tuple-element.23), channel_id=1, source_target_pairs={{0,240},{1,241},{2,242},{3,243},{4,244},{5,245},{6,246},{7,247},{8... | collective-permute-start | bytes 196616 | tf_op jit(solution)/shard_map/ppermute | solution.py:371
  42.3 4.0 %collective-permute-start.2 = (f32[16,1024]{1,0:T(8,128)S(1)}, f32[16,1024]{1,0:T(8,128)S(1)}, u32[]{:S(2)}, u32[]{:S(2)}) collective-permute-start(f32[16,1024]{1,0:T(8,128)S(1)} %get-tuple-element.24), channel_id=1, source_target_pairs={{0,192},{1,193},{2,194},{3,195},{4,196},{5,197},{6,198},{7,199},{8... | collective-permute-start | bytes 196616 | tf_op jit(solution)/shard_map/ppermute | solution.py:371
  42.4 4.2 %collective-permute-start.3 = (f32[16,1024]{1,0:T(8,128)S(1)}, f32[16,1024]{1,0:T(8,128)S(1)}, u32[]{:S(2)}, u32[]{:S(2)}) collective-permute-start(f32[16,1024]{1,0:T(8,128)S(1)} %get-tuple-element.25), channel_id=1, source_target_pairs={{0,48},{1,49},{2,50},{3,51},{4,52},{5,53},{6,54},{7,55},{8,24},{9,... | collective-permute-start | bytes 196616 | tf_op jit(solution)/shard_map/ppermute | solution.py:371
  46.6 9.0 %collective-permute-start.4 = (f32[16,1024]{1,0:T(8,128)S(1)}, f32[16,1024]{1,0:T(8,128)S(1)}, u32[]{:S(2)}, u32[]{:S(2)}) collective-permute-start(f32[16,1024]{1,0:T(8,128)S(1)} %add_add_fusion.1), channel_id=1, source_target_pairs={{0,4},{1,5},{2,6},{3,7},{4,0},{5,1},{6,2},{7,3},{8,12},{9,13},{10,... | collective-permute-start | bytes 196616 | tf_op jit(solution)/shard_map/ppermute | solution.py:371
  48.6 7.8 %collective-permute-start.5 = (f32[16,1024]{1,0:T(8,128)S(1)}, f32[16,1024]{1,0:T(8,128)S(1)}, u32[]{:S(2)}, u32[]{:S(2)}) collective-permute-start(f32[16,1024]{1,0:T(8,128)S(1)} %add_add_fusion.1), channel_id=1, source_target_pairs={{0,3},{1,6},{2,5},{3,0},{4,7},{5,2},{6,1},{7,4},{8,13},{9,12},{10,... | collective-permute-start | bytes 196616 | tf_op jit(solution)/shard_map/ppermute | solution.py:371
  48.6 7.8 %collective-permute-start.6 = (f32[16,1024]{1,0:T(8,128)S(1)}, f32[16,1024]{1,0:T(8,128)S(1)}, u32[]{:S(2)}, u32[]{:S(2)}) collective-permute-start(f32[16,1024]{1,0:T(8,128)S(1)} %add_add_fusion.1), channel_id=1, source_target_pairs={{0,7},{1,2},{2,1},{3,4},{4,3},{5,6},{6,5},{7,0},{8,9},{9,8},{10,11... | collective-permute-start | bytes 196616 | tf_op jit(solution)/shard_map/ppermute | solution.py:371
  56.4 3.4 %collective-permute-start.7 = (f32[16,1024]{1,0:T(8,128)S(1)}, f32[16,1024]{1,0:T(8,128)S(1)}, u32[]{:S(2)}, u32[]{:S(2)}) collective-permute-start(f32[16,1024]{1,0:T(8,128)S(1)} %add_add_fusion.refs_0_), channel_id=1, source_target_pairs={{0,48},{1,49},{2,50},{3,51},{4,52},{5,53},{6,54},{7,55},{8,24},{9,... | collective-permute-start | bytes 196616 | tf_op jit(solution)/shard_map/ppermute | solution.py:371
  57.6 3.1 %collective-permute-start.8 = (f32[16,1024]{1,0:T(8,128)S(1)}, f32[16,1024]{1,0:T(8,128)S(1)}, u32[]{:S(2)}, u32[]{:S(2)}) collective-permute-start(f32[16,1024]{1,0:T(8,128)S(1)} %add_add_fusion.refs_0_), channel_id=1, source_target_pairs={{0,192},{1,193},{2,194},{3,195},{4,196},{5,197},{6,198},{7,199},{8... | collective-permute-start | bytes 196616 | tf_op jit(solution)/shard_map/ppermute | solution.py:371
  58.3 4.0 %collective-permute-start.9 = (f32[16,1024]{1,0:T(8,128)S(1)}, f32[16,1024]{1,0:T(8,128)S(1)}, u32[]{:S(2)}, u32[]{:S(2)}) collective-permute-start(f32[16,1024]{1,0:T(8,128)S(1)} %add_add_fusion.refs_0_), channel_id=1, source_target_pairs={{0,240},{1,241},{2,242},{3,243},{4,244},{5,245},{6,246},{7,247},{8... | collective-permute-start | bytes 196616 | tf_op jit(solution)/shard_map/ppermute | solution.py:371
  62.5 26.2 %copy-start.2 = (bf16[512,1024]{1,0:T(8,128)(2,1)S(1)}, bf16[512,1024]{1,0:T(8,128)(2,1)}, u32[]{:S(2)}) copy-start(bf16[512,1024]{1,0:T(8,128)(2,1)} %get-tuple-element.35.words_hbm) | copy-start | bytes 3145732
  84.3 8.2 %collective-permute-start.10 = (f32[512,1024]{1,0:T(8,128)S(1)}, f32[512,1024]{1,0:T(8,128)}, u32[]{:S(2)}, u32[]{:S(2)}) collective-permute-start(f32[512,1024]{1,0:T(8,128)S(1)} %bitcast.10), channel_id=1, source_target_pairs={{0,8},{1,9},{2,10},{3,11},{4,12},{5,13},{6,14},{7,15},{8,0},{9,1},... | collective-permute-start | bytes 6291464 | tf_op jit(solution)/shard_map/ppermute | solution.py:371

commit v6 on v5

--- a/solution.py
+++ b/solution.py
@@ -34,7 +34,7 @@
         words[s * width:(s + 1) * width, :] = nn(books[s], hot).astype(BF)
 
 
-def first_kernel(scale, half_ref, mine_ref, codes_hbm, books_hbm, corpus_hbm, out, words_hbm, codes, books, corpus, words, sems):
+def first_kernel(scale, half_ref, mine_ref, codes_hbm, books_hbm, corpus_hbm, out, words_hbm, corpus, codes, books, words, sems):
     subs = books.shape[0]
     first = pl.multiple_of(half_ref[0] * subs, subs)
     tables = []
@@ -65,12 +65,11 @@
     return pl.pallas_call(
         functools.partial(first_kernel, scale),
         in_specs=[pl.BlockSpec(memory_space=pltpu.SMEM)] * 2 + [pl.BlockSpec(memory_space=pl.ANY)] * 3,
-        out_specs=[pl.BlockSpec(memory_space=pltpu.VMEM), pl.BlockSpec(memory_space=pltpu.HBM)],
-        out_shape=[jax.ShapeDtypeStruct((part * width, d), F32), pltpu.HBM((part * width, rows), BF)],
+        out_specs=[pl.BlockSpec(memory_space=pltpu.VMEM), pl.BlockSpec(memory_space=pltpu.HBM), pl.BlockSpec(memory_space=pltpu.VMEM)],
+        out_shape=[jax.ShapeDtypeStruct((part * width, d), F32), pltpu.HBM((part * width, rows), BF), jax.ShapeDtypeStruct((rows, d), BF)],
         scratch_shapes=[
             pltpu.VMEM((part, rows), jnp.int32),
             pltpu.VMEM((part, width, size), BF),
-            pltpu.VMEM((rows, d), BF),
             pltpu.VMEM((part * width, rows), BF),
             pltpu.SemaphoreType.DMA((2 + 2 * (part // CHUNK),)),
         ],
@@ -151,19 +150,18 @@
     )(mine, *parts)
 
 
-def dist_kernel(half_ref, sums_ref, rot_hbm, corpus_hbm, words_hbm, out_ref, rot, corpus, words, sems):
+def dist_kernel(half_ref, sums_ref, corpus_ref, rot_hbm, words_hbm, out_ref, rot, words, sems):
     cols = words.shape[0]
     first = pl.multiple_of(half_ref[0] * cols, cols)
     loads = [
-        pltpu.make_async_copy(corpus_hbm, corpus, sems.at[0]),
-        pltpu.make_async_copy(rot_hbm.at[:, pl.ds(first, cols)], rot, sems.at[1]),
-        pltpu.make_async_copy(words_hbm, words, sems.at[2]),
+        pltpu.make_async_copy(rot_hbm.at[:, pl.ds(first, cols)], rot, sems.at[0]),
+        pltpu.make_async_copy(words_hbm, words, sems.at[1]),
     ]
     for load in loads:
         load.start()
     for load in loads:
         load.wait()
-    rotated = lax.dot_general(rot[...], corpus[...], (((0,), (1,)), ((), ())), preferred_element_type=F32)
+    rotated = lax.dot_general(rot[...], corpus_ref[...], (((0,), (1,)), ((), ())), preferred_element_type=F32)
     gap = rotated - words[...].astype(F32)
     out_ref[...] = sums_ref[...] + jnp.sum(gap * gap, axis=0, keepdims=True)
 
@@ -173,18 +171,17 @@
     cols = words.shape[0]
     return pl.pallas_call(
         dist_kernel,
-        in_specs=[pl.BlockSpec(memory_space=pltpu.SMEM), pl.BlockSpec(memory_space=pltpu.VMEM)] + [pl.BlockSpec(memory_space=pl.ANY)] * 3,
+        in_specs=[pl.BlockSpec(memory_space=pltpu.SMEM), pl.BlockSpec(memory_space=pltpu.VMEM), pl.BlockSpec(memory_space=pltpu.VMEM)] + [pl.BlockSpec(memory_space=pl.ANY)] * 2,
         out_specs=pl.BlockSpec(memory_space=pltpu.VMEM),
         out_shape=jax.ShapeDtypeStruct((1, rows), F32),
         scratch_shapes=[
             pltpu.VMEM((d, cols), BF),
-            pltpu.VMEM((rows, d), BF),
             pltpu.VMEM((cols, rows), BF),
-            pltpu.SemaphoreType.DMA((3,)),
+            pltpu.SemaphoreType.DMA((2,)),
         ],
         compiler_params=pltpu.CompilerParams(vmem_limit_bytes=24 * MIB),
         name="distortion",
-    )(half, sums, rotation, corpus, words)
+    )(half, sums, corpus, rotation, words)
 
 
 def polar_polynomial(steps):
@@ -394,9 +391,9 @@
     scale = 1.0 / math.sqrt(rows * lax.axis_size("gx") * lax.axis_size("gy"))
 
     far_half, near_half = (1 - core).reshape(1), core.reshape(1)
-    far_term, far_words = cross_half(far_half, mine, held[0], held[1], held[2], scale)
+    far_term, far_words, near_corpus = cross_half(far_half, mine, held[0], held[1], held[2], scale)
     arrived = send(far_term, SWAP_CORE)
-    near_term, near_words = cross_second(near_half, codes_t, books_t, corpus, scale)
+    near_term, near_words = cross_second(near_half, codes_t, books_t, near_corpus, scale)
 
     groups = cube_groups()
     members = len(groups[0])
@@ -407,7 +404,7 @@
     part = part + got[0] + got[1] + got[2]
     part, far_words = lax.optimization_barrier((part, far_words))
     others = [send(part, pairs) for pairs in (SWAP_BOTH, SWAP_FAR, SWAP_Z)]
-    gaps = distortion(far_half, jnp.zeros((1, rows), F32), held[3], held[2], far_words)
+    gaps = distortion(far_half, jnp.zeros((1, rows), F32), held[3], near_corpus, far_words)
     others, gaps = lax.optimization_barrier((others, gaps))
     part = part + others[0] + others[1] + others[2]
     got = [send(part, p) for p in (SWAP_XY, SWAP_Y, SWAP_X)]
@@ -416,7 +413,7 @@
     own = own.reshape(-1, d)
     own, near_words = lax.optimization_barrier((own, near_words))
     other = send(own, SWAP_CORE)
-    gaps = distortion(near_half, gaps, held[3], held[2], near_words)
+    gaps = distortion(near_half, gaps, held[3], near_corpus, near_words)
     other, gaps = lax.optimization_barrier((other, gaps))
     place = jnp.stack([core, gx // 4, gx % 4])
     return polar(place, own, other), gaps.reshape(rows)

time: 113 us -> 114 us (level)
  waiting for transfers between devices: 5.78 us -> 8.8 us
  starting transfers between devices: 19 us -> 17.3 us
    ppermute x11, waiting for transfers between devices: 5.78 us -> 8.8 us  [send(): return lax.ppermute(value, AXES, pairs)]
    ppermute x11, starting transfers between devices: 19 us -> 17.3 us  [send(): return lax.ppermute(value, AXES, pairs)]
    pallas_call x2, Pallas kernels: 6.97 us -> 5.69 us  [distortion(): pl.pallas_call(dist_kernel, in_specs=[pl.BlockSpec(memory_space=pltpu.SME...]
  transfers between devices with their start and end apart: 11 -> 11, of which waited for: 7 -> 8; matrix products, arithmetic and copies ran while one was open for 0% -> 0% of each run, Pallas kernels for 9% -> 8%
where the time goes in v6:
time: 114 us
  blocking collectives  51.5 us (45%)
  Pallas kernels  34.8 us (31%)
  starting transfers between devices  17.3 us (15%)
  waiting for transfers between devices  8.8 us (8%)
    all_to_all x1, blocking collectives, body(): pieces = lax.all_to_all(summed, AXES, 0, 0, axis_index_groups=groups)  28.9 us
    all_to_all x1, blocking collectives, body(): own = lax.all_to_all(gathered, AXES, 0, 0, axis_index_groups=groups)  22.6 us
    pallas_call x1, Pallas kernels, polar(): pl.pallas_call(functools.partial(polar_kernel, polar_polynomial(ITERS)),...  20.7 us
    ppermute x11, starting transfers between devices, send(): return lax.ppermute(value, AXES, pairs)  17.3 us
    ppermute x11, waiting for transfers between devices, send(): return lax.ppermute(value, AXES, pairs)  8.8 us
    pallas_call x2, Pallas kernels, distortion(): pl.pallas_call(dist_kernel, in_specs=[pl.BlockSpec(memory_space=pltpu.SME...  5.69 us
    pallas_call x1, Pallas kernels, cross_half(): pl.pallas_call(functools.partial(first_kernel, scale), in_specs=[pl.Block...  4.73 us
    pallas_call x1, Pallas kernels, cross_second(): pl.pallas_call(functools.partial(second_kernel, scale), in_specs=[pl.Bloc...  3.45 us
  transfers between devices with their start and end apart: 11, of which 8 were waited for; matrix products, arithmetic and copies ran while one was open for 0% of the time, Pallas kernels for 8%

profile of v6, /device:TPU:1, one launch (start us, length us, event | category | flops | bytes accessed | tf_op | source)
XLA Modules:
  0.0 114.0 jit_solution(11661510714880163327)
XLA Ops:
  0.7 4.7 %cross_half.1 = (f32[512,1024]{1,0:T(8,128)S(1)}, bf16[512,1024]{1,0:T(8,128)(2,1)}, bf16[1024,1024]{1,0:T(8,128)(2,1)S(1)}) custom-call(s32[1]{0:T(128)} %bitcast.6.half_ref, s32[1]{0:T(128)} %bitcast.3.mine_ref, s32[64,1024]{1,0:T(8,128)} %bitcast.12, bf16[64,16,256]{2,1,0:T(8,128)(2,1)} %bitcast.10, bf16[1024,1024]{1,0:T(8,128)(2,1)} %corpus_hbm.1), custom_call_target="tpu_custom_call" | custom-call | tf_op jit(solution)/shard_map/cross_half/pallas_call | solution.py:65
  5.5 3.3 %collective-permute-start = (f32[512,1024]{1,0:T(8,128)S(1)}, f32[512,1024]{1,0:T(8,128)S(1)}, u32[]{:S(2)}, u32[]{:S(2)}) collective-permute-start(f32[512,1024]{1,0:T(8,128)S(1)} %get-tuple-element.23), channel_id=1, source_target_pairs={{0,8},{1,9},{2,10},{3,11},{4,12},{5,13},{6,14},{7,15},{8,0},{9,1},... | collective-permute-start | bytes 6291464 | tf_op jit(solution)/shard_map/ppermute | solution.py:368
  8.8 3.5 %cross_second.1 = (f32[512,1024]{1,0:T(8,128)S(1)}, bf16[512,1024]{1,0:T(8,128)(2,1)}) custom-call(s32[1]{0:T(128)} %bitcast.half_ref, s32[64,1024]{1,0:T(8,128)S(1)} %bitcast.13, bf16[64,16,256]{2,1,0:T(8,128)(2,1)S(1)} %bitcast.11, bf16[1024,1024]{1,0:T(8,128)(2,1)S(1)} %get-tuple-element.21.corpus_ref), custom_call_target="tpu_custom_call" | custom-call | tf_op jit(solution)/shard_map/cross_second/pallas_call | solution.py:99
  12.2 0.3 collective-permute-done
  12.6 0.5 add.45
  13.1 28.9 %all_to_all.10.pieces_ref = f32[8,64,1024]{2,1,0:T(8,128)S(1)} all-to-all(f32[8,64,1024]{2,1,0:T(8,128)S(1)} %bitcast.14), channel_id=1, replica_groups={{0,1,16,17,64,65,80,81},{3,2,19,18,67,66,83,82},{4,5,20,21,68,69,84,85}..., dimensions={0} | all-to-all | bytes 4194304 | tf_op jit(solution)/shard_map/all_to_all | solution.py:401
  42.3 2.5 %collective-permute-start.3 = (f32[16,1024]{1,0:T(8,128)S(1)}, f32[16,1024]{1,0:T(8,128)S(1)}, u32[]{:S(2)}, u32[]{:S(2)}) collective-permute-start(f32[16,1024]{1,0:T(8,128)S(1)} %get-tuple-element.27), channel_id=1, source_target_pairs={{0,48},{1,49},{2,50},{3,51},{4,52},{5,53},{6,54},{7,55},{8,24},{9,... | collective-permute-start | bytes 196616 | tf_op jit(solution)/shard_map/ppermute | solution.py:368
  44.9 1.4 %collective-permute-done.1 = f32[16,1024]{1,0:T(8,128)S(1)} collective-permute-done((f32[16,1024]{1,0:T(8,128)S(1)}, f32[16,1024]{1,0:T(8,128)S(1)}, u32[]{:S(2)}, u32[]{:S(2)}) %collective-permute-start.1) | collective-permute-done | bytes 65568 | tf_op jit(solution)/shard_map/ppermute | solution.py:368
  46.2 0.3 collective-permute-done.3
  46.6 2.1 %collective-permute-start.5 = (f32[16,1024]{1,0:T(8,128)S(1)}, f32[16,1024]{1,0:T(8,128)S(1)}, u32[]{:S(2)}, u32[]{:S(2)}) collective-permute-start(f32[16,1024]{1,0:T(8,128)S(1)} %add_add_fusion.1), channel_id=1, source_target_pairs={{0,3},{1,6},{2,5},{3,0},{4,7},{5,2},{6,1},{7,4},{8,13},{9,12},{10,... | collective-permute-start | bytes 196616 | tf_op jit(solution)/shard_map/ppermute | solution.py:368
  48.8 3.5 %collective-permute-start.4 = (f32[16,1024]{1,0:T(8,128)S(1)}, f32[16,1024]{1,0:T(8,128)S(1)}, u32[]{:S(2)}, u32[]{:S(2)}) collective-permute-start(f32[16,1024]{1,0:T(8,128)S(1)} %add_add_fusion.1), channel_id=1, source_target_pairs={{0,4},{1,5},{2,6},{3,7},{4,0},{5,1},{6,2},{7,3},{8,12},{9,13},{10,... | collective-permute-start | bytes 196616 | tf_op jit(solution)/shard_map/ppermute | solution.py:368
  52.3 2.6 %distortion.2.sums_ref = f32[1,1024]{1,0:T(1,128)S(1)} custom-call(s32[1]{0:T(128)} %bitcast.6.half_ref, f32[1,1024]{1,0:T(1,128)S(1)} %broadcast_in_dim.3.sums_ref, bf16[1024,1024]{1,0:T(8,128)(2,1)S(1)} %get-tuple-element.21.corpus_ref, bf16[1024,1024]{1,0:T(8,128)(2,1)} %rot_hbm.3, bf16[512,1024]{1,0:T(8,128)(2,1)S(1)} %copy-done.2), custom_call_target="tpu_custom_call" | custom-call | tf_op jit(solution)/shard_map/distortion/pallas_call | solution.py:172
  54.9 2.8 %collective-permute-done.4 = f32[16,1024]{1,0:T(8,128)S(1)} collective-permute-done((f32[16,1024]{1,0:T(8,128)S(1)}, f32[16,1024]{1,0:T(8,128)S(1)}, u32[]{:S(2)}, u32[]{:S(2)}) %collective-permute-start.4) | collective-permute-done | bytes 65568 | tf_op jit(solution)/shard_map/ppermute | solution.py:368
  57.7 0.4 collective-permute-start.9
  58.1 2.9 %collective-permute-start.8 = (f32[16,1024]{1,0:T(8,128)S(1)}, f32[16,1024]{1,0:T(8,128)S(1)}, u32[]{:S(2)}, u32[]{:S(2)}) collective-permute-start(f32[16,1024]{1,0:T(8,128)S(1)} %add_add_fusion.refs_0_), channel_id=1, source_target_pairs={{0,192},{1,193},{2,194},{3,195},{4,196},{5,197},{6,198},{7,199},{8... | collective-permute-start | bytes 196616 | tf_op jit(solution)/shard_map/ppermute | solution.py:368
  61.0 0.9 collective-permute-done.9.refs_3_
  62.0 0.7 collective-permute-done.8.refs_2_
  62.7 1.5 %collective-permute-done.7.refs_1_ = f32[16,1024]{1,0:T(8,128)S(1)} collective-permute-done((f32[16,1024]{1,0:T(8,128)S(1)}, f32[16,1024]{1,0:T(8,128)S(1)}, u32[]{:S(2)}, u32[]{:S(2)}) %collective-permute-start.7) | collective-permute-done | bytes 65568 | tf_op jit(solution)/shard_map/ppermute | solution.py:368
  64.2 0.1 spread.1
  64.3 22.6 %all_to_all.11 = f32[8,64,1024]{2,1,0:T(8,128)} all-to-all(f32[8,64,1024]{2,1,0:T(8,128)S(1)} %spread.1), channel_id=1, replica_groups={{0,1,16,17,64,65,80,81},{3,2,19,18,67,66,83,82},{4,5,20,21,68,69,84,85}..., dimensions={0} | all-to-all | bytes 4194304 | tf_op jit(solution)/shard_map/all_to_all | solution.py:412
  86.9 2.1 %collective-permute-start.10 = (f32[512,1024]{1,0:T(8,128)}, f32[512,1024]{1,0:T(8,128)}, u32[]{:S(2)}, u32[]{:S(2)}) collective-permute-start(f32[512,1024]{1,0:T(8,128)} %bitcast.8.own_ref), channel_id=1, source_target_pairs={{0,8},{1,9},{2,10},{3,11},{4,12},{5,13},{6,14},{7,15},{8,0},{9,1},... | collective-permute-start | bytes 6291464 | tf_op jit(solution)/shard_map/ppermute | solution.py:368
  89.1 3.1 %distortion.3 = f32[1,1024]{1,0:T(1,128)} custom-call(s32[1]{0:T(128)} %bitcast.half_ref, f32[1,1024]{1,0:T(1,128)S(1)} %distortion.2.sums_ref, bf16[1024,1024]{1,0:T(8,128)(2,1)S(1)} %get-tuple-element.21.corpus_ref, bf16[1024,1024]{1,0:T(8,128)(2,1)} %rot_hbm.3, bf16[512,1024]{1,0:T(8,128)(2,1)S(1)} %copy-done.1), custom_call_target="tpu_custom_call" | custom-call | tf_op jit(solution)/shard_map/distortion/pallas_call | solution.py:172
  92.2 0.9 collective-permute-done.10.oth_hbm
  93.1 20.7 %polar.1 = f32[32,1024]{1,0:T(8,128)} custom-call(s32[3]{0:T(128)S(1)} %pad_add_fusion.place_ref, f32[512,1024]{1,0:T(8,128)} %bitcast.8.own_ref, f32[512,1024]{1,0:T(8,128)} %collective-permute-done.10.oth_hbm), custom_call_target="tpu_custom_call" | custom-call | tf_op jit(solution)/shard_map/polar/pallas_call | solution.py:294
  (20 shorter events, 0.5 us)
Async XLA Ops:
  0.6 8.2 %copy-start = (bf16[64,256,16]{1,2,0:T(8,128)(2,1)S(1)}, bf16[64,256,16]{1,2,0:T(8,128)(2,1)}, u32[]{:S(2)}) copy-start(bf16[64,256,16]{1,2,0:T(8,128)(2,1)} %param.7) | copy-start | bytes 1572868
  0.6 8.1 %copy-start.3 = (s32[1024,64]{0,1:T(8,128)S(1)}, s32[1024,64]{0,1:T(8,128)}, u32[]{:S(2)}) copy-start(s32[1024,64]{0,1:T(8,128)} %param.6) | copy-start | bytes 786436
  5.5 7.1 %collective-permute-start = (f32[512,1024]{1,0:T(8,128)S(1)}, f32[512,1024]{1,0:T(8,128)S(1)}, u32[]{:S(2)}, u32[]{:S(2)}) collective-permute-start(f32[512,1024]{1,0:T(8,128)S(1)} %get-tuple-element.23), channel_id=1, source_target_pairs={{0,8},{1,9},{2,10},{3,11},{4,12},{5,13},{6,14},{7,15},{8,0},{9,1},... | collective-permute-start | bytes 6291464 | tf_op jit(solution)/shard_map/ppermute | solution.py:368
  42.0 10.3 %copy-start.2 = (bf16[512,1024]{1,0:T(8,128)(2,1)S(1)}, bf16[512,1024]{1,0:T(8,128)(2,1)}, u32[]{:S(2)}) copy-start(bf16[512,1024]{1,0:T(8,128)(2,1)} %get-tuple-element.30.words_hbm) | copy-start | bytes 3145732
  42.1 4.1 %collective-permute-start.1 = (f32[16,1024]{1,0:T(8,128)S(1)}, f32[16,1024]{1,0:T(8,128)S(1)}, u32[]{:S(2)}, u32[]{:S(2)}) collective-permute-start(f32[16,1024]{1,0:T(8,128)S(1)} %get-tuple-element.25), channel_id=1, source_target_pairs={{0,240},{1,241},{2,242},{3,243},{4,244},{5,245},{6,246},{7,247},{8... | collective-permute-start | bytes 196616 | tf_op jit(solution)/shard_map/ppermute | solution.py:368
  42.2 4.0 %collective-permute-start.2 = (f32[16,1024]{1,0:T(8,128)S(1)}, f32[16,1024]{1,0:T(8,128)S(1)}, u32[]{:S(2)}, u32[]{:S(2)}) collective-permute-start(f32[16,1024]{1,0:T(8,128)S(1)} %get-tuple-element.26), channel_id=1, source_target_pairs={{0,192},{1,193},{2,194},{3,195},{4,196},{5,197},{6,198},{7,199},{8... | collective-permute-start | bytes 196616 | tf_op jit(solution)/shard_map/ppermute | solution.py:368
  42.3 4.2 %collective-permute-start.3 = (f32[16,1024]{1,0:T(8,128)S(1)}, f32[16,1024]{1,0:T(8,128)S(1)}, u32[]{:S(2)}, u32[]{:S(2)}) collective-permute-start(f32[16,1024]{1,0:T(8,128)S(1)} %get-tuple-element.27), channel_id=1, source_target_pairs={{0,48},{1,49},{2,50},{3,51},{4,52},{5,53},{6,54},{7,55},{8,24},{9,... | collective-permute-start | bytes 196616 | tf_op jit(solution)/shard_map/ppermute | solution.py:368
  46.5 8.3 %collective-permute-start.6 = (f32[16,1024]{1,0:T(8,128)S(1)}, f32[16,1024]{1,0:T(8,128)S(1)}, u32[]{:S(2)}, u32[]{:S(2)}) collective-permute-start(f32[16,1024]{1,0:T(8,128)S(1)} %add_add_fusion.1), channel_id=1, source_target_pairs={{0,7},{1,2},{2,1},{3,4},{4,3},{5,6},{6,5},{7,0},{8,9},{9,8},{10,11... | collective-permute-start | bytes 196616 | tf_op jit(solution)/shard_map/ppermute | solution.py:368
  46.6 8.2 %collective-permute-start.5 = (f32[16,1024]{1,0:T(8,128)S(1)}, f32[16,1024]{1,0:T(8,128)S(1)}, u32[]{:S(2)}, u32[]{:S(2)}) collective-permute-start(f32[16,1024]{1,0:T(8,128)S(1)} %add_add_fusion.1), channel_id=1, source_target_pairs={{0,3},{1,6},{2,5},{3,0},{4,7},{5,2},{6,1},{7,4},{8,13},{9,12},{10,... | collective-permute-start | bytes 196616 | tf_op jit(solution)/shard_map/ppermute | solution.py:368
  48.8 8.9 %collective-permute-start.4 = (f32[16,1024]{1,0:T(8,128)S(1)}, f32[16,1024]{1,0:T(8,128)S(1)}, u32[]{:S(2)}, u32[]{:S(2)}) collective-permute-start(f32[16,1024]{1,0:T(8,128)S(1)} %add_add_fusion.1), channel_id=1, source_target_pairs={{0,4},{1,5},{2,6},{3,7},{4,0},{5,1},{6,2},{7,3},{8,12},{9,13},{10,... | collective-permute-start | bytes 196616 | tf_op jit(solution)/shard_map/ppermute | solution.py:368
  57.7 4.3 %collective-permute-start.9 = (f32[16,1024]{1,0:T(8,128)S(1)}, f32[16,1024]{1,0:T(8,128)S(1)}, u32[]{:S(2)}, u32[]{:S(2)}) collective-permute-start(f32[16,1024]{1,0:T(8,128)S(1)} %add_add_fusion.refs_0_), channel_id=1, source_target_pairs={{0,240},{1,241},{2,242},{3,243},{4,244},{5,245},{6,246},{7,247},{8... | collective-permute-start | bytes 196616 | tf_op jit(solution)/shard_map/ppermute | solution.py:368
  58.1 4.6 %collective-permute-start.8 = (f32[16,1024]{1,0:T(8,128)S(1)}, f32[16,1024]{1,0:T(8,128)S(1)}, u32[]{:S(2)}, u32[]{:S(2)}) collective-permute-start(f32[16,1024]{1,0:T(8,128)S(1)} %add_add_fusion.refs_0_), channel_id=1, source_target_pairs={{0,192},{1,193},{2,194},{3,195},{4,196},{5,197},{6,198},{7,199},{8... | collective-permute-start | bytes 196616 | tf_op jit(solution)/shard_map/ppermute | solution.py:368
  61.0 3.1 %collective-permute-start.7 = (f32[16,1024]{1,0:T(8,128)S(1)}, f32[16,1024]{1,0:T(8,128)S(1)}, u32[]{:S(2)}, u32[]{:S(2)}) collective-permute-start(f32[16,1024]{1,0:T(8,128)S(1)} %add_add_fusion.refs_0_), channel_id=1, source_target_pairs={{0,48},{1,49},{2,50},{3,51},{4,52},{5,53},{6,54},{7,55},{8,24},{9,... | collective-permute-start | bytes 196616 | tf_op jit(solution)/shard_map/ppermute | solution.py:368
  64.3 24.8 %copy-start.1 = (bf16[512,1024]{1,0:T(8,128)(2,1)S(1)}, bf16[512,1024]{1,0:T(8,128)(2,1)}, u32[]{:S(2)}) copy-start(bf16[512,1024]{1,0:T(8,128)(2,1)} %get-tuple-element.37.words_hbm) | copy-start | bytes 3145732
  86.9 6.2 %collective-permute-start.10 = (f32[512,1024]{1,0:T(8,128)}, f32[512,1024]{1,0:T(8,128)}, u32[]{:S(2)}, u32[]{:S(2)}) collective-permute-start(f32[512,1024]{1,0:T(8,128)} %bitcast.8.own_ref), channel_id=1, source_target_pairs={{0,8},{1,9},{2,10},{3,11},{4,12},{5,13},{6,14},{7,15},{8,0},{9,1},... | collective-permute-start | bytes 6291464 | tf_op jit(solution)/shard_map/ppermute | solution.py:368
